TPU v7x, 128 devices: a whole 4x4x4 slice. The times are simulated.
128 devices in a mesh: row: 16 (over x, y_lo, core), col: 4 (over z), layer: 2 (over y_hi).
Axes of the slice: x: 4, y: 4 (y_hi: 2, y_lo: 2; y = y_hi * 2 + y_lo), z: 4, core: 2. Of those that a mesh axis runs over, the one named last changes fastest.
Arguments:
- a_blocks: bfloat16 [16, 4, 2, 12, 256, 256], P('row', 'col', 'layer'), may hold values from -6 to 6
- b_blocks: bfloat16 [16, 4, 2, 32, 256, 256], P('row', 'col', 'layer'), may hold values from -0.375 to 0.375
- a_offsets: int32 [24, 4, 12], P(None, 'col'), may hold values from -8 to 7, as said below
- b_offsets: int32 [256, 12], replicated, may hold values from -8 to 7, as said below
- keep_offsets: int32 [24, 4, 16], P(None, 'col', 'row'), may hold values from -16 to 15, as said below
- owners: int32 [24, 4, 16], P('layer', 'col', 'row'), may hold values from 0 to 3, as said below
Outputs:
- next_blocks: bfloat16 [16, 4, 2, 4, 6, 256, 256], P('row', 'col', 'layer')
Inputs may be any that keep to these rules, and one draw needn't show every extreme that they name: `a_offsets`: the 12 offsets of each row are distinct. `b_offsets`: the 12 offsets of each row are distinct. keep_offsets[t, c, r] is congruent to r - c - 4 t modulo 16. Among the 12 values of owners[t, c, r] with t in one half [l * 12, (l + 1) * 12), at most 6 are equal; for every l and r one owner is named exactly 6 times for every c.
All inputs are finite; a program needn't handle non-finite values.
Results may differ from a plain program's by a relative error of at most 0.0042.
Values may be sent and summed in bfloat16 or wider, within the bound.
A program may use at most 192 MiB of HBM per device.

v0:
```python
import jax
import jax.numpy as jnp
from jax import lax
from jax.sharding import PartitionSpec as P


def passed_along(value, axis, by):
    count = lax.axis_size(axis)
    return lax.ppermute(value, axis, [(i, (i + by) % count) for i in range(count)])


def piece_plan(
    group_index,
    target,
    piece_id,
    row_offsets,
    b_offsets,
    band_width,
    pieces,
    groups,
    held_pieces,
    group_rows,
    side_blocks,
    kept_offsets,
):
    period = pieces // groups
    residues = jnp.arange(period, dtype=jnp.int32)
    inside = (
        jnp.remainder(piece_id - group_index - groups * residues + band_width // 2, pieces)
        < band_width
    )
    ranked = jnp.argsort(jnp.where(inside, residues, residues + period))[:held_pieces]
    periods = jnp.arange(group_rows // period, dtype=jnp.int32)
    tile_rows = (periods[:, None] * period + ranked[None, :]).reshape(-1)
    matrix_row = group_index + groups * tile_rows
    offset_a = jnp.remainder(piece_id - matrix_row + band_width // 2, pieces) - band_width // 2
    column_k = jnp.remainder(matrix_row + offset_a, side_blocks)
    piece_row = (column_k - piece_id) // pieces
    offset_b = jnp.remainder(target - column_k + band_width // 2, band_width) - band_width // 2
    a_present = jnp.any(row_offsets[tile_rows] == offset_a[:, None], axis=1)
    b_present = jnp.any(b_offsets[column_k] == offset_b[:, None], axis=1)
    kept_cell = kept_offsets[tile_rows] == offset_a + offset_b
    return (ranked, piece_row, a_present & b_present & kept_cell)


def pass_rows(a_current):
    return passed_along(a_current, "row", -1)


def on_device(a_blocks, b_blocks, a_offsets, b_offsets, keep_offsets, owners):
    band_width = lax.axis_size("row")
    groups = lax.axis_size("col")
    layers = lax.axis_size("layer")
    target = lax.axis_index("row")
    group_index = lax.axis_index("col")
    layer_index = lax.axis_index("layer")
    share_rows = a_blocks.shape[3]
    block_size = a_blocks.shape[5]
    held_pieces = band_width // groups
    pieces = layers * band_width
    piece_rows = b_blocks.shape[3] // held_pieces
    side_blocks = piece_rows * pieces
    group_rows = a_offsets.shape[0]
    period = pieces // groups
    windows = group_rows // period
    row_offsets = a_offsets[:, 0, :]
    kept_offsets = keep_offsets[:, 0, 0]
    first_piece = target + held_pieces * group_index
    residue_ids = jnp.arange(period, dtype=jnp.int32)
    piece_ids = jnp.arange(piece_rows, dtype=jnp.int32)

    def add_piece(total, a_current, b_current, slot_base, piece_id):
        ranked, piece_row, weight = piece_plan(
            group_index,
            target,
            piece_id,
            row_offsets,
            b_offsets,
            band_width,
            pieces,
            groups,
            held_pieces,
            group_rows,
            side_blocks,
            kept_offsets,
        )
        slab = lax.dynamic_slice_in_dim(b_current, slot_base, piece_rows, 0)
        picker = (piece_row[:, None] == piece_ids[None, :]).astype(jnp.bfloat16)
        chosen = jnp.einsum("sk,kab->sab", picker, slab, preferred_element_type=jnp.float32).astype(
            jnp.bfloat16
        )
        products = jnp.einsum("sab,sbc->sac", a_current, chosen, preferred_element_type=jnp.float32)
        products = products.reshape(windows, held_pieces, block_size, block_size)
        placing = (ranked[:, None] == residue_ids[None, :]).astype(jnp.float32)
        placing = (
            weight.astype(jnp.float32).reshape(windows, held_pieces)[:, :, None]
            * placing[None, :, :]
        )
        added = jnp.einsum("wgab,wgu->wuab", products, placing, precision=lax.Precision.HIGHEST)
        return total + added.reshape(group_rows, block_size, block_size)

    empty = jnp.zeros((group_rows, block_size, block_size), jnp.float32)
    a_part = a_blocks.reshape(share_rows, block_size, block_size)
    b_held = b_blocks.reshape(held_pieces * piece_rows, block_size, block_size)
    total = empty
    for round_index in range(groups):

        def inner(step_index, carry):
            running, a_current = carry
            piece_seq = jnp.remainder(
                first_piece + round_index * held_pieces + step_index, band_width
            )
            running = add_piece(
                running,
                a_current,
                b_held,
                step_index * piece_rows,
                layer_index * band_width + piece_seq,
            )
            return (running, pass_rows(a_current))

        total, a_part = lax.fori_loop(0, held_pieces - 1, inner, (total, a_part))
        last_seq = jnp.remainder(
            first_piece + round_index * held_pieces + held_pieces - 1, band_width
        )
        total = add_piece(
            total,
            a_part,
            b_held,
            (held_pieces - 1) * piece_rows,
            layer_index * band_width + last_seq,
        )
        if round_index + 1 < groups:
            a_part = pass_rows(a_part)
            b_held = passed_along(b_held, "col", -1)
    halves = lax.psum_scatter(total.astype(jnp.bfloat16), "layer", scatter_dimension=0, tiled=True)
    products = halves
    owner_cols = owners[:, 0, 0]
    send_slots = share_rows // 2
    one_hot = (owner_cols[:, None] == jnp.arange(groups, dtype=jnp.int32)[None, :]).astype(
        jnp.int32
    )
    order_rank = jnp.sum(jnp.cumsum(one_hot, axis=0) * one_hot, axis=1) - 1
    position = owner_cols * send_slots + order_rank
    placement = (
        jnp.arange(groups * send_slots, dtype=jnp.int32)[:, None] == position[None, :]
    ).astype(jnp.bfloat16)
    outgoing = jnp.einsum(
        "os,sab->oab", placement, products, preferred_element_type=jnp.float32
    ).astype(jnp.bfloat16)
    outgoing = outgoing.reshape(groups, send_slots, block_size, block_size)
    arrived = lax.all_to_all(outgoing, "col", split_axis=0, concat_axis=0, tiled=True)
    return arrived.reshape(1, 1, 1, groups, send_slots, block_size, block_size)


def solution(mesh):
    return jax.shard_map(
        on_device,
        mesh=mesh,
        in_specs=(
            P("row", "col", "layer", None, None, None),
            P("row", "col", "layer", None, None, None),
            P(None, "col", None),
            P(),
            P(None, "col", "row"),
            P("layer", "col", "row"),
        ),
        out_specs=P("row", "col", "layer", None, None, None, None),
        check_vma=False,
    )
```

profile of v0, /device:TPU:8, one launch (start us, length us, event | category | flops | bytes accessed | tf_op | source)
XLA Modules:
  0.0 609.3 jit_solution(2066795108392876784)
XLA Ops:
  20.7 96.0 %while.87 = (s32[]{:T(128)}, f32[24,256,256]{2,1,0:T(8,128)}, bf16[12,256,256]{2,1,0:T(8,128)(2,1)}, s32[]{:T(128)}, s32[]{:T(128)}, /*index=5*/s32[]{:T(128)}, ...) while((s32[]{:T(128)}, f32[24,256,256]{2,1,0:T(8,128)}, ...), condition=%wide.region_6.7_spmd.clone.clone, body=%wide.region_2.6_spmd.clone.clone.sunk | while | flops 494670464 | bytes 65550164 | solution.py:122
  36.5 7.0 %fusion.393 = f32[3,8,256,256]{3,1,2,0:T(8,128)S(1)} fusion(f32[3,4,256,256]{3,1,2,0:T(4,128)S(1)} %copy.149, f32[4,8]{1,0:T(4,128)S(1)} %fusion.391, f32[3,4]{1,0:T(4,128)S(1)} %and_convert_fusion.15), kind=kOutput, calls=%fused_computation.272.clone.1 | convolution fusion | flops 75497568 | bytes 9437360 | tf_op jit(solution)/shard_map/while/body/eval_jaxpr/wgab,wgu->wuab/dot_general | solution.py:99
  66.1 7.0 %fusion.393 = f32[3,8,256,256]{3,1,2,0:T(8,128)S(1)} fusion(f32[3,4,256,256]{3,1,2,0:T(4,128)S(1)} %copy.149, f32[4,8]{1,0:T(4,128)S(1)} %fusion.391, f32[3,4]{1,0:T(4,128)S(1)} %and_convert_fusion.15), kind=kOutput, calls=%fused_computation.272.clone.1 | convolution fusion | flops 75497568 | bytes 9437360 | tf_op jit(solution)/shard_map/while/body/eval_jaxpr/wgab,wgu->wuab/dot_general | solution.py:99
  75.1 6.9 %bitcast_add_fusion.15 = f32[24,256,256]{2,1,0:T(8,128)} fusion(f32[3,8,256,256]{3,2,1,0:T(8,128)S(1)} %copy.150, f32[24,256,256]{2,1,0:T(8,128)} %get-tuple-element.2801, pred[]{:T(512)S(6)} %compare.411), kind=kLoop, calls=%fused_computation.265.clone.1 | loop fusion | flops 3145728 | bytes 18874368 | tf_op jit(solution)/shard_map/while/body/eval_jaxpr/add | solution.py:100
  100.8 7.0 %fusion.393 = f32[3,8,256,256]{3,1,2,0:T(8,128)S(1)} fusion(f32[3,4,256,256]{3,1,2,0:T(4,128)S(1)} %copy.149, f32[4,8]{1,0:T(4,128)S(1)} %fusion.391, f32[3,4]{1,0:T(4,128)S(1)} %and_convert_fusion.15), kind=kOutput, calls=%fused_computation.272.clone.1 | convolution fusion | flops 75497568 | bytes 9437360 | tf_op jit(solution)/shard_map/while/body/eval_jaxpr/wgab,wgu->wuab/dot_general | solution.py:99
  137.0 7.8 %fusion.151 = f32[3,8,256,256]{3,1,2,0:T(8,128)S(1)} fusion(f32[3,4,256,256]{3,2,1,0:T(8,128)S(1)} %bitcast.242, f32[4,8]{1,0:T(4,128)S(1)} %fusion.233, f32[3,4]{1,0:T(4,128)S(1)} %get-tuple-element.2410), kind=kOutput, calls=%fused_computation.355 | convolution fusion | flops 75497568 | bytes 9437360 | tf_op jit(solution)/shard_map/wgab,wgu->wuab/dot_general | solution.py:99
  151.8 8.3 %bitcast_add_fusion.7 = f32[24,256,256]{2,1,0:T(8,128)} fusion(f32[24,256,256]{2,1,0:T(8,128)} %get-tuple-element.1887, f32[3,8,256,256]{3,2,1,0:T(8,128)} %copy.72), kind=kLoop, calls=%fused_computation.348 | loop fusion | flops 1572864 | bytes 18874368 | tf_op jit(solution)/shard_map/add | solution.py:100
  160.7 95.3 %while.84 = (s32[]{:T(128)}, f32[24,256,256]{2,1,0:T(8,128)}, bf16[12,256,256]{2,1,0:T(8,128)(2,1)}, s32[]{:T(128)}, s32[]{:T(128)}, /*index=5*/s32[]{:T(128)}, ...) while((s32[]{:T(128)}, f32[24,256,256]{2,1,0:T(8,128)}, ...), condition=%wide.region_14.15_spmd.clone.clone, body=%wide.region_10.14_spmd.clone.clone.sunk | while | flops 493097600 | bytes 65550156 | solution.py:122
  176.6 7.0 %fusion.360 = f32[3,8,256,256]{3,1,2,0:T(8,128)S(1)} fusion(f32[3,4,256,256]{3,1,2,0:T(4,128)S(1)} %copy.140, f32[4,8]{1,0:T(4,128)S(1)} %fusion.358, f32[3,4]{1,0:T(4,128)S(1)} %and_convert_fusion.12), kind=kOutput, calls=%fused_computation.35.clone.1 | convolution fusion | flops 75497568 | bytes 9437360 | tf_op jit(solution)/shard_map/while/body/eval_jaxpr/wgab,wgu->wuab/dot_general | solution.py:99
  208.5 7.0 %fusion.360 = f32[3,8,256,256]{3,1,2,0:T(8,128)S(1)} fusion(f32[3,4,256,256]{3,1,2,0:T(4,128)S(1)} %copy.140, f32[4,8]{1,0:T(4,128)S(1)} %fusion.358, f32[3,4]{1,0:T(4,128)S(1)} %and_convert_fusion.12), kind=kOutput, calls=%fused_computation.35.clone.1 | convolution fusion | flops 75497568 | bytes 9437360 | tf_op jit(solution)/shard_map/while/body/eval_jaxpr/wgab,wgu->wuab/dot_general | solution.py:99
  240.5 7.0 %fusion.360 = f32[3,8,256,256]{3,1,2,0:T(8,128)S(1)} fusion(f32[3,4,256,256]{3,1,2,0:T(4,128)S(1)} %copy.140, f32[4,8]{1,0:T(4,128)S(1)} %fusion.358, f32[3,4]{1,0:T(4,128)S(1)} %and_convert_fusion.12), kind=kOutput, calls=%fused_computation.35.clone.1 | convolution fusion | flops 75497568 | bytes 9437360 | tf_op jit(solution)/shard_map/while/body/eval_jaxpr/wgab,wgu->wuab/dot_general | solution.py:99
  262.0 7.8 %fusion.149 = f32[3,8,256,256]{3,1,2,0:T(8,128)S(1)} fusion(f32[3,4,256,256]{3,2,1,0:T(8,128)S(1)} %bitcast.243, f32[4,8]{1,0:T(4,128)S(1)} %fusion.234, f32[3,4]{1,0:T(4,128)S(1)} %get-tuple-element.2408), kind=kOutput, calls=%fused_computation.353 | convolution fusion | flops 75497568 | bytes 9437360 | tf_op jit(solution)/shard_map/wgab,wgu->wuab/dot_general | solution.py:99
  276.3 98.3 %while.85 = (s32[]{:T(128)}, f32[24,256,256]{2,1,0:T(8,128)}, bf16[12,256,256]{2,1,0:T(8,128)(2,1)}, s32[]{:T(128)}, s32[]{:T(128)}, /*index=5*/s32[]{:T(128)}, ...) while((s32[]{:T(128)}, f32[24,256,256]{2,1,0:T(8,128)}, ...), condition=%wide.region_22.23_spmd.clone.clone, body=%wide.region_18.22_spmd.clone.clone.sunk | while | flops 493097600 | bytes 65550156 | solution.py:122
  293.7 7.0 %fusion.371 = f32[3,8,256,256]{3,1,2,0:T(8,128)S(1)} fusion(f32[3,4,256,256]{3,1,2,0:T(4,128)S(1)} %copy.143, f32[4,8]{1,0:T(4,128)S(1)} %fusion.369, f32[3,4]{1,0:T(4,128)S(1)} %and_convert_fusion.13), kind=kOutput, calls=%fused_computation.114.clone.1 | convolution fusion | flops 75497568 | bytes 9437360 | tf_op jit(solution)/shard_map/while/body/eval_jaxpr/wgab,wgu->wuab/dot_general | solution.py:99
  325.1 7.0 %fusion.371 = f32[3,8,256,256]{3,1,2,0:T(8,128)S(1)} fusion(f32[3,4,256,256]{3,1,2,0:T(4,128)S(1)} %copy.143, f32[4,8]{1,0:T(4,128)S(1)} %fusion.369, f32[3,4]{1,0:T(4,128)S(1)} %and_convert_fusion.13), kind=kOutput, calls=%fused_computation.114.clone.1 | convolution fusion | flops 75497568 | bytes 9437360 | tf_op jit(solution)/shard_map/while/body/eval_jaxpr/wgab,wgu->wuab/dot_general | solution.py:99
  359.1 7.0 %fusion.371 = f32[3,8,256,256]{3,1,2,0:T(8,128)S(1)} fusion(f32[3,4,256,256]{3,1,2,0:T(4,128)S(1)} %copy.143, f32[4,8]{1,0:T(4,128)S(1)} %fusion.369, f32[3,4]{1,0:T(4,128)S(1)} %and_convert_fusion.13), kind=kOutput, calls=%fused_computation.114.clone.1 | convolution fusion | flops 75497568 | bytes 9437360 | tf_op jit(solution)/shard_map/while/body/eval_jaxpr/wgab,wgu->wuab/dot_general | solution.py:99
  379.2 7.8 %fusion.147 = f32[3,8,256,256]{3,1,2,0:T(8,128)S(1)} fusion(f32[3,4,256,256]{3,2,1,0:T(8,128)S(1)} %bitcast.244, f32[4,8]{1,0:T(4,128)S(1)} %copy-done.4, f32[3,4]{1,0:T(4,128)S(1)} %copy-done.2), kind=kOutput, calls=%fused_computation.351 | convolution fusion | flops 75497568 | bytes 9437360 | tf_op jit(solution)/shard_map/wgab,wgu->wuab/dot_general | solution.py:99
  396.6 95.7 %while.86 = (s32[]{:T(128)}, f32[24,256,256]{2,1,0:T(8,128)}, bf16[12,256,256]{2,1,0:T(8,128)(2,1)}, s32[]{:T(128)}, s32[]{:T(128)}, /*index=5*/s32[]{:T(128)}, ...) while((s32[]{:T(128)}, f32[24,256,256]{2,1,0:T(8,128)}, ...), condition=%wide.region_30.31_spmd.clone.clone, body=%wide.region_26.30_spmd.clone.clone.sunk | while | flops 493097600 | bytes 65550156 | solution.py:122
  412.9 7.0 %fusion.382 = f32[3,8,256,256]{3,1,2,0:T(8,128)S(1)} fusion(f32[3,4,256,256]{3,1,2,0:T(4,128)S(1)} %copy.146, f32[4,8]{1,0:T(4,128)S(1)} %fusion.380, f32[3,4]{1,0:T(4,128)S(1)} %and_convert_fusion.14), kind=kOutput, calls=%fused_computation.193.clone.1 | convolution fusion | flops 75497568 | bytes 9437360 | tf_op jit(solution)/shard_map/while/body/eval_jaxpr/wgab,wgu->wuab/dot_general | solution.py:99
  444.3 7.0 %fusion.382 = f32[3,8,256,256]{3,1,2,0:T(8,128)S(1)} fusion(f32[3,4,256,256]{3,1,2,0:T(4,128)S(1)} %copy.146, f32[4,8]{1,0:T(4,128)S(1)} %fusion.380, f32[3,4]{1,0:T(4,128)S(1)} %and_convert_fusion.14), kind=kOutput, calls=%fused_computation.193.clone.1 | convolution fusion | flops 75497568 | bytes 9437360 | tf_op jit(solution)/shard_map/while/body/eval_jaxpr/wgab,wgu->wuab/dot_general | solution.py:99
  476.7 7.0 %fusion.382 = f32[3,8,256,256]{3,1,2,0:T(8,128)S(1)} fusion(f32[3,4,256,256]{3,1,2,0:T(4,128)S(1)} %copy.146, f32[4,8]{1,0:T(4,128)S(1)} %fusion.380, f32[3,4]{1,0:T(4,128)S(1)} %and_convert_fusion.14), kind=kOutput, calls=%fused_computation.193.clone.1 | convolution fusion | flops 75497568 | bytes 9437360 | tf_op jit(solution)/shard_map/while/body/eval_jaxpr/wgab,wgu->wuab/dot_general | solution.py:99
  495.3 8.0 %fusion.145 = f32[3,8,256,256]{3,1,2,0:T(8,128)S(1)} fusion(f32[3,4,256,256]{3,2,1,0:T(8,128)S(1)} %bitcast.241, f32[4,8]{1,0:T(4,128)S(1)} %copy-done.3, f32[3,4]{1,0:T(4,128)S(1)} %copy-done.1), kind=kOutput, calls=%fused_computation.349 | convolution fusion | flops 75497568 | bytes 9437360 | tf_op jit(solution)/shard_map/wgab,wgu->wuab/dot_general | solution.py:99
  509.2 46.2 %reduce-scatter.2.cloned.1.call-done = bf16[12,256,256]{2,1,0:T(8,128)(2,1)} async-done(((bf16[24,256,256]{2,1,0:T(8,128)(2,1)}), bf16[12,256,256]{2,1,0:T(8,128)(2,1)}) %reduce-scatter.2.cloned.1.call-update) | async-done | bytes 1572880 | tf_op jit(solution)/shard_map/reduce_scatter | solution.py:136
  558.8 41.8 %all_to_all.5 = bf16[4,6,256,256]{3,2,1,0:T(8,128)(2,1)S(1)} all-to-all(bf16[4,6,256,256]{3,2,1,0:T(8,128)(2,1)S(1)} %bitcast.245), channel_id=1, replica_groups=mesh['row'=16,'col'=4,'layer'=2] {'col'}, dimensions={0} | all-to-all | bytes 6291456 | tf_op jit(solution)/shard_map/all_to_all | solution.py:152
  (498 shorter events, 375.3 us)
Async XLA Ops:
  6.5 548.9 %reduce-scatter.2.cloned.1.call-start = ((), (), s32[]{:S(2)}) async-start(), calls=%async_computation.2 | async-start | bytes 4718592 | tf_op jit(solution)/shard_map/reduce_scatter | solution.py:136
  9.3 11.4 %copy-start = (s32[24,1,1]{0,2,1:T(1,128)S(1)}, s32[24,1,1]{0,2,1:T(1,128)}, u32[]{:S(2)}) copy-start(s32[24,1,1]{0,2,1:T(1,128)} %param.18) | copy-start | bytes 292
  15.9 144.2 %collective-permute-start.5 = (bf16[32,256,256]{2,0,1:T(8,128)(2,1)}, bf16[32,256,256]{2,0,1:T(8,128)(2,1)}, u32[]{:S(2)}, u32[]{:S(2)}) collective-permute-start(bf16[32,256,256]{2,0,1:T(8,128)(2,1)} %bitcast.144.clone.2), channel_id=1, source_target_pairs={{0,6},{2,0},{4,2},{6,4},{1,7},{3,1},{5,3},{7,5},{8,14},{10,8},{12,... | collective-permute-start | bytes 12582920 | tf_op jit(solution)/shard_map/ppermute | solution.py:9
  23.4 26.3 %collective-permute-start.3 = (bf16[12,256,256]{2,1,0:T(8,128)(2,1)}, bf16[12,256,256]{2,1,0:T(8,128)(2,1)}, u32[]{:S(2)}, u32[]{:S(2)}) collective-permute-start(bf16[12,256,256]{2,1,0:T(8,128)(2,1)} %copy.156), channel_id=1, source_target_pairs={{0,120},{8,0},{16,8},{24,16},{32,24},{40,32},{48,40},{56,48},{64,5... | collective-permute-start | bytes 4718600 | tf_op jit(solution)/shard_map/while/body/eval_jaxpr/ppermute | solution.py:9
  52.3 29.7 %collective-permute-start.3 = (bf16[12,256,256]{2,1,0:T(8,128)(2,1)}, bf16[12,256,256]{2,1,0:T(8,128)(2,1)}, u32[]{:S(2)}, u32[]{:S(2)}) collective-permute-start(bf16[12,256,256]{2,1,0:T(8,128)(2,1)} %copy.156), channel_id=1, source_target_pairs={{0,120},{8,0},{16,8},{24,16},{32,24},{40,32},{48,40},{56,48},{64,5... | collective-permute-start | bytes 4718600 | tf_op jit(solution)/shard_map/while/body/eval_jaxpr/ppermute | solution.py:9
  84.7 32.0 %collective-permute-start.3 = (bf16[12,256,256]{2,1,0:T(8,128)(2,1)}, bf16[12,256,256]{2,1,0:T(8,128)(2,1)}, u32[]{:S(2)}, u32[]{:S(2)}) collective-permute-start(bf16[12,256,256]{2,1,0:T(8,128)(2,1)} %copy.156), channel_id=1, source_target_pairs={{0,120},{8,0},{16,8},{24,16},{32,24},{40,32},{48,40},{56,48},{64,5... | collective-permute-start | bytes 4718600 | tf_op jit(solution)/shard_map/while/body/eval_jaxpr/ppermute | solution.py:9
  116.7 44.0 %collective-permute-start.4 = (bf16[12,256,256]{2,1,0:T(8,128)(2,1)}, bf16[12,256,256]{2,1,0:T(8,128)(2,1)}, u32[]{:S(2)}, u32[]{:S(2)}) collective-permute-start(bf16[12,256,256]{2,1,0:T(8,128)(2,1)} %get-tuple-element.1889), channel_id=1, source_target_pairs={{0,120},{8,0},{16,8},{24,16},{32,24},{40,32},{48,40},{56,48},{64,5... | collective-permute-start | bytes 4718600 | tf_op jit(solution)/shard_map/ppermute | solution.py:9
  160.1 115.9 %collective-permute-start.7 = (bf16[32,256,256]{2,0,1:T(8,128)(2,1)}, bf16[32,256,256]{2,0,1:T(8,128)(2,1)}, u32[]{:S(2)}, u32[]{:S(2)}) collective-permute-start(bf16[32,256,256]{2,0,1:T(8,128)(2,1)} %collective-permute-done.5), channel_id=1, source_target_pairs={{0,6},{2,0},{4,2},{6,4},{1,7},{3,1},{5,3},{7,5},{8,14},{10,8},{12,... | collective-permute-start | bytes 12582920 | tf_op jit(solution)/shard_map/ppermute | solution.py:9
  163.4 28.7 %collective-permute-start = (bf16[12,256,256]{2,1,0:T(8,128)(2,1)}, bf16[12,256,256]{2,1,0:T(8,128)(2,1)}, u32[]{:S(2)}, u32[]{:S(2)}) collective-permute-start(bf16[12,256,256]{2,1,0:T(8,128)(2,1)} %copy.165), channel_id=1, source_target_pairs={{0,120},{8,0},{16,8},{24,16},{32,24},{40,32},{48,40},{56,48},{64,5... | collective-permute-start | bytes 4718600 | tf_op jit(solution)/shard_map/while/body/eval_jaxpr/ppermute | solution.py:9
  194.7 29.3 %collective-permute-start = (bf16[12,256,256]{2,1,0:T(8,128)(2,1)}, bf16[12,256,256]{2,1,0:T(8,128)(2,1)}, u32[]{:S(2)}, u32[]{:S(2)}) collective-permute-start(bf16[12,256,256]{2,1,0:T(8,128)(2,1)} %copy.165), channel_id=1, source_target_pairs={{0,120},{8,0},{16,8},{24,16},{32,24},{40,32},{48,40},{56,48},{64,5... | collective-permute-start | bytes 4718600 | tf_op jit(solution)/shard_map/while/body/eval_jaxpr/ppermute | solution.py:9
  226.6 29.4 %collective-permute-start = (bf16[12,256,256]{2,1,0:T(8,128)(2,1)}, bf16[12,256,256]{2,1,0:T(8,128)(2,1)}, u32[]{:S(2)}, u32[]{:S(2)}) collective-permute-start(bf16[12,256,256]{2,1,0:T(8,128)(2,1)} %copy.165), channel_id=1, source_target_pairs={{0,120},{8,0},{16,8},{24,16},{32,24},{40,32},{48,40},{56,48},{64,5... | collective-permute-start | bytes 4718600 | tf_op jit(solution)/shard_map/while/body/eval_jaxpr/ppermute | solution.py:9
  256.0 20.2 %collective-permute-start.6 = (bf16[12,256,256]{2,1,0:T(8,128)(2,1)}, bf16[12,256,256]{2,1,0:T(8,128)(2,1)}, u32[]{:S(2)}, u32[]{:S(2)}) collective-permute-start(bf16[12,256,256]{2,1,0:T(8,128)(2,1)} %get-tuple-element.1892), channel_id=1, source_target_pairs={{0,120},{8,0},{16,8},{24,16},{32,24},{40,32},{48,40},{56,48},{64,5... | collective-permute-start | bytes 4718600 | tf_op jit(solution)/shard_map/ppermute | solution.py:9
  259.6 12.2 %slice-start = ((s8[6291456]{0:T(1024)(128)(4,1)}), s8[4194304]{0:T(1024)(128)(4,1)S(1)}, s32[]{:S(2)}) async-start(s8[6291456]{0:T(1024)(128)(4,1)} %bitcast.234), calls=%async_computation.3 | async-start | bytes 8388608
  276.0 117.2 %collective-permute-start.9 = (bf16[32,256,256]{2,0,1:T(8,128)(2,1)}, bf16[32,256,256]{2,0,1:T(8,128)(2,1)}, u32[]{:S(2)}, u32[]{:S(2)}) collective-permute-start(bf16[32,256,256]{2,0,1:T(8,128)(2,1)} %collective-permute-done.7), channel_id=1, source_target_pairs={{0,6},{2,0},{4,2},{6,4},{1,7},{3,1},{5,3},{7,5},{8,14},{10,8},{12,... | collective-permute-start | bytes 12582920 | tf_op jit(solution)/shard_map/ppermute | solution.py:9
  276.3 98.5 %copy-start.9 = (s32[12]{0:T(128)S(1)}, s32[12]{0:T(128)}, u32[]{:S(2)}) copy-start(s32[12]{0:T(128)} %and_select_fusion.35) | copy-start | bytes 148
  279.0 30.2 %collective-permute-start.1 = (bf16[12,256,256]{2,1,0:T(8,128)(2,1)}, bf16[12,256,256]{2,1,0:T(8,128)(2,1)}, u32[]{:S(2)}, u32[]{:S(2)}) collective-permute-start(bf16[12,256,256]{2,1,0:T(8,128)(2,1)} %copy.174), channel_id=1, source_target_pairs={{0,120},{8,0},{16,8},{24,16},{32,24},{40,32},{48,40},{56,48},{64,5... | collective-permute-start | bytes 4718600 | tf_op jit(solution)/shard_map/while/body/eval_jaxpr/ppermute | solution.py:9
  311.9 28.7 %collective-permute-start.1 = (bf16[12,256,256]{2,1,0:T(8,128)(2,1)}, bf16[12,256,256]{2,1,0:T(8,128)(2,1)}, u32[]{:S(2)}, u32[]{:S(2)}) collective-permute-start(bf16[12,256,256]{2,1,0:T(8,128)(2,1)} %copy.174), channel_id=1, source_target_pairs={{0,120},{8,0},{16,8},{24,16},{32,24},{40,32},{48,40},{56,48},{64,5... | collective-permute-start | bytes 4718600 | tf_op jit(solution)/shard_map/while/body/eval_jaxpr/ppermute | solution.py:9
  343.2 31.4 %collective-permute-start.1 = (bf16[12,256,256]{2,1,0:T(8,128)(2,1)}, bf16[12,256,256]{2,1,0:T(8,128)(2,1)}, u32[]{:S(2)}, u32[]{:S(2)}) collective-permute-start(bf16[12,256,256]{2,1,0:T(8,128)(2,1)} %copy.174), channel_id=1, source_target_pairs={{0,120},{8,0},{16,8},{24,16},{32,24},{40,32},{48,40},{56,48},{64,5... | collective-permute-start | bytes 4718600 | tf_op jit(solution)/shard_map/while/body/eval_jaxpr/ppermute | solution.py:9
  374.6 22.0 %collective-permute-start.8 = (bf16[12,256,256]{2,1,0:T(8,128)(2,1)}, bf16[12,256,256]{2,1,0:T(8,128)(2,1)}, u32[]{:S(2)}, u32[]{:S(2)}) collective-permute-start(bf16[12,256,256]{2,1,0:T(8,128)(2,1)} %get-tuple-element.1895), channel_id=1, source_target_pairs={{0,120},{8,0},{16,8},{24,16},{32,24},{40,32},{48,40},{56,48},{64,5... | collective-permute-start | bytes 4718600 | tf_op jit(solution)/shard_map/ppermute | solution.py:9
  376.8 12.3 %slice-start.2 = ((s8[6291456]{0:T(1024)(128)(4,1)}), s8[4194304]{0:T(1024)(128)(4,1)S(1)}, s32[]{:S(2)}) async-start(s8[6291456]{0:T(1024)(128)(4,1)} %bitcast.236), calls=%async_computation.5 | async-start | bytes 8388608
  399.7 28.7 %collective-permute-start.2 = (bf16[12,256,256]{2,1,0:T(8,128)(2,1)}, bf16[12,256,256]{2,1,0:T(8,128)(2,1)}, u32[]{:S(2)}, u32[]{:S(2)}) collective-permute-start(bf16[12,256,256]{2,1,0:T(8,128)(2,1)} %copy.183), channel_id=1, source_target_pairs={{0,120},{8,0},{16,8},{24,16},{32,24},{40,32},{48,40},{56,48},{64,5... | collective-permute-start | bytes 4718600 | tf_op jit(solution)/shard_map/while/body/eval_jaxpr/ppermute | solution.py:9
  431.1 28.7 %collective-permute-start.2 = (bf16[12,256,256]{2,1,0:T(8,128)(2,1)}, bf16[12,256,256]{2,1,0:T(8,128)(2,1)}, u32[]{:S(2)}, u32[]{:S(2)}) collective-permute-start(bf16[12,256,256]{2,1,0:T(8,128)(2,1)} %copy.183), channel_id=1, source_target_pairs={{0,120},{8,0},{16,8},{24,16},{32,24},{40,32},{48,40},{56,48},{64,5... | collective-permute-start | bytes 4718600 | tf_op jit(solution)/shard_map/while/body/eval_jaxpr/ppermute | solution.py:9
  462.6 29.7 %collective-permute-start.2 = (bf16[12,256,256]{2,1,0:T(8,128)(2,1)}, bf16[12,256,256]{2,1,0:T(8,128)(2,1)}, u32[]{:S(2)}, u32[]{:S(2)}) collective-permute-start(bf16[12,256,256]{2,1,0:T(8,128)(2,1)} %copy.183), channel_id=1, source_target_pairs={{0,120},{8,0},{16,8},{24,16},{32,24},{40,32},{48,40},{56,48},{64,5... | collective-permute-start | bytes 4718600 | tf_op jit(solution)/shard_map/while/body/eval_jaxpr/ppermute | solution.py:9
  492.3 13.1 %slice-start.4 = ((s8[6291456]{0:T(1024)(128)(4,1)}), s8[4194304]{0:T(1024)(128)(4,1)S(1)}, s32[]{:S(2)}) async-start(s8[6291456]{0:T(1024)(128)(4,1)} %bitcast.238), calls=%async_computation.7 | async-start | bytes 8388608
  (11 other events, 67.9 us)
Sparse Core Ops, SparseCore 0:
  508.5 46.8 reduce-scatter.1
where the time goes:
time: 616 us; the launch traced here: 609 us
  matrix products  212 us (34%)
  local copies, waits for them, and re-layouts  153 us (25%)
  other arithmetic  123 us (20%)
  waiting for transfers between devices  46.3 us (8%)
  blocking collectives  41.8 us (7%)
  starting transfers between devices  18.3 us (3%)
  between operations  14.1 us (2%)
    dot_general x16, matrix products, add_piece(): jnp.einsum('wgab,wgu->wuab', products, placing, precision=lax.Precision.H...  115 us
    add x15, other arithmetic, add_piece(): return total + added.reshape(group_rows, block_size, block_size)  92.7 us
    dot_general x16, matrix products, add_piece(): jnp.einsum('sab,sbc->sac', a_current, chosen, preferred_element_type=jnp....  60.8 us
    reduce_scatter x1, waiting for transfers between devices, on_device(): lax.psum_scatter(total.astype(jnp.bfloat16), 'layer', scatter_dimension=0...  46.2 us
    all_to_all x1, blocking collectives, on_device(): lax.all_to_all(outgoing, 'col', split_axis=0, concat_axis=0, tiled=True)  41.8 us
    reshape x12, local copies, waits for them, and re-layouts, add_piece(): products = products.reshape(windows, held_pieces, block_size, block_size)  39.2 us
    dot_general x16, local copies, waits for them, and re-layouts, add_piece(): jnp.einsum('wgab,wgu->wuab', products, placing, precision=lax.Precision.H...  34.9 us
    dot_general x16, matrix products, add_piece(): jnp.einsum('sk,kab->sab', picker, slab, preferred_element_type=jnp.float32)  33 us
  transfers between devices with their start and end apart: 19, of which 1 were waited for; matrix products, arithmetic and copies ran while one was open for 74% of the time, Pallas kernels for 0%

commit v1 on v0

v1 whole, which is shorter than its diff:
```python
import functools

import jax
import jax.numpy as jnp
from jax import lax
from jax.experimental import pallas as pl
from jax.experimental.pallas import tpu as pltpu
from jax.sharding import PartitionSpec as P

MESH = pl.DeviceIdType.MESH
BLOCK = 256
PHASES = 3
NX = 2


def mod(value, count):
    return lax.rem(value + 32 * count, jnp.int32(count))


def kernel(
    a_ref,
    b_ref,
    a_mask,
    b_mask,
    keep,
    slot_source,
    slot_used,
    out_ref,
    abuf,
    bbuf,
    total,
    mine,
    outgoing_part,
    incoming_part,
    slots,
    local_sem,
    a_send,
    b_send,
    p_send,
    o_send,
    x_recv,
    x2_recv,
    xy_recv,
    yy_recv,
    yx_recv,
    yx2_recv,
    core_recv,
    bz_recv,
    bz2_recv,
    p_recv,
    o_recv,
):
    r = lax.axis_index("row")
    c = lax.axis_index("col")
    l = lax.axis_index("layer")
    x, y, b = r // 4, (r // 2) % 2, r % 2

    def row_of(xx, yy, bb):
        return xx * 4 + yy * 2 + bb

    xp, xm, x2 = mod(x + 1, 4), mod(x - 1, 4), mod(x + 2, 4)
    zp, zm, z2 = mod(c + 1, 4), mod(c - 1, 4), mod(c + 2, 4)
    y1, b1, l1 = 1 - y, 1 - b, 1 - l
    to_xp, to_xm = {"row": row_of(xp, y, b)}, {"row": row_of(xm, y, b)}
    to_y, to_b = {"row": row_of(x, y1, b)}, {"row": row_of(x, y, b1)}
    to_zp, to_zm, to_z2 = {"col": zp}, {"col": zm}, {"col": z2}
    to_l = {"layer": l1}

    barrier = pltpu.get_barrier_semaphore()
    for device in (to_xp, to_xm, to_y, to_b, to_zp, to_zm, to_z2, to_l):
        pl.semaphore_signal(barrier, inc=1, device_id=device, device_id_type=MESH)
    pl.semaphore_wait(barrier, 8)

    def remote(src, dst, send, recv, device):
        return pltpu.make_async_remote_copy(
            src_ref=src, dst_ref=dst, send_sem=send, recv_sem=recv, device_id=device, device_id_type=MESH
        )

    def third(phase):
        return lax.rem(2 * phase, jnp.int32(3))

    def blocks(source, phase, first, count):
        return abuf.at[source, pl.ds(third(phase) * 4 + first, count)]

    def pass_a(source, phase, first, count, recv, device):
        ref = blocks(source, phase, first, count)
        remote(ref, ref, a_send.at[phase], recv, device).start()

    def got_a(source, phase, first, count, recv):
        ref = blocks(source, phase, first, count)
        remote(ref, ref, a_send.at[phase], recv, to_b).wait_recv()

    ny = 4 - NX
    half = NX // 2
    hy = ny // 2

    def own_copy(phase):
        return pltpu.make_async_copy(
            a_ref.at[pl.ds(third(phase) * 4, 4)], blocks(r, phase, 0, 4), local_sem.at[phase]
        )

    def b_own_copy(part):
        return pltpu.make_async_copy(
            b_ref.at[:, mod(part - l, 8)], bbuf.at[c, part], local_sem.at[PHASES + part]
        )

    def send_own(phase):
        own_copy(phase).wait()
        pass_a(r, phase, NX, ny, yy_recv.at[phase], to_y)
        pass_a(r, phase, 0, NX, x_recv.at[phase, 0], to_xp)
        pass_a(r, phase, 0, NX, x_recv.at[phase, 1], to_xm)
        pass_a(r, phase, NX, ny, yx_recv.at[phase, 0, 0], to_xp)
        pass_a(r, phase, NX, ny, yx_recv.at[phase, 0, 1], to_xm)
        pass_a(r, phase, 0, NX, xy_recv.at[phase, 0], to_y)
        pass_a(r, phase, 0, 4, core_recv.at[phase, 0], to_b)

    def pass_b(source, part, first, count, recv, device):
        ref = bbuf.at[source, part, pl.ds(first, count)]
        remote(ref, ref, b_send.at[part], recv, device).start()

    def got_b(source, part, first, count, recv):
        ref = bbuf.at[source, part, pl.ds(first, count)]
        remote(ref, ref, b_send.at[part], recv, to_zp).wait_recv()

    def send_own_b(part):
        b_own_copy(part).wait()
        pass_b(c, part, 0, 4, bz_recv.at[part, 0], to_zp)
        pass_b(c, part, 0, 4, bz_recv.at[part, 1], to_zm)

    def forward_b(part):
        got_b(zm, part, 0, 4, bz_recv.at[part, 0])
        pass_b(zm, part, 0, 2, bz2_recv.at[part, 0], to_zp)
        got_b(zp, part, 0, 4, bz_recv.at[part, 1])
        pass_b(zp, part, 2, 2, bz2_recv.at[part, 1], to_zm)

    def last_b(part):
        got_b(z2, part, 0, 2, bz2_recv.at[part, 0])
        got_b(z2, part, 2, 2, bz2_recv.at[part, 1])

    def multiply(source, phase):
        piece = 16 * l + mod(source + 4 * c, 16)
        top = mod(piece - c + 8, 32) // 4
        for g in range(4):
            u = jnp.where(top >= 3, top - 3 + g, jnp.where(g <= top, g, g + 4))
            t = 8 * third(phase) + u
            i = c + 4 * t
            d = mod(piece - i + 8, 32) - 8
            k = mod(i + d, 256)
            part = mod(k // 32 + l, 8)
            e = mod(r - k + 8, 16) - 8
            distance = mod(k - r, 16)
            present = (
                lax.shift_right_logical(a_mask[t], d + 8) & lax.shift_right_logical(b_mask[k], e + 8) & 1
            )
            weight = jnp.where(keep[t] == d + e, present, 0).astype(jnp.float32)
            product = jnp.dot(
                abuf[source, third(phase) * 4 + g],
                bbuf[distance // 4, part, distance % 4],
                preferred_element_type=jnp.float32,
            )
            total[u] += product * weight

    for phase in range(PHASES):
        own_copy(phase).start()
    for part in range(4):
        b_own_copy(part).start()
    send_own(0)
    send_own_b(0)
    send_own_b(1)

    def run_phase(phase, carry):
        s = row_of(x, y1, b)
        got_a(s, phase, NX, ny, yy_recv.at[phase])
        pass_a(s, phase, NX, ny, yx_recv.at[phase, 1, 0], to_xp)
        pass_a(s, phase, NX, ny, yx_recv.at[phase, 1, 1], to_xm)

        @pl.when(phase < 2)
        def _():
            part = 2 * phase
            forward_b(part)

        s = row_of(xm, y, b)
        got_a(s, phase, 0, NX, x_recv.at[phase, 0])
        pass_a(s, phase, 0, half, x2_recv.at[phase, 0], to_xp)
        pass_a(s, phase, 0, NX, xy_recv.at[phase, 1], to_y)
        s = row_of(xp, y, b)
        got_a(s, phase, 0, NX, x_recv.at[phase, 1])
        pass_a(s, phase, half, NX - half, x2_recv.at[phase, 1], to_xm)
        pass_a(s, phase, 0, NX, xy_recv.at[phase, 2], to_y)
        for index, yy in ((0, y), (1, y1)):
            s = row_of(xm, yy, b)
            got_a(s, phase, NX, ny, yx_recv.at[phase, index, 0])
            pass_a(s, phase, NX, hy, yx2_recv.at[phase, index, 0], to_xp)
            s = row_of(xp, yy, b)
            got_a(s, phase, NX, ny, yx_recv.at[phase, index, 1])
            pass_a(s, phase, NX + hy, ny - hy, yx2_recv.at[phase, index, 1], to_xm)

        @pl.when(phase < 2)
        def _():
            send_own(phase + 1)

        @pl.when(phase < 1)
        def _():
            send_own_b(2)
            send_own_b(3)

        s = row_of(x2, y, b)
        got_a(s, phase, 0, half, x2_recv.at[phase, 0])
        got_a(s, phase, half, NX - half, x2_recv.at[phase, 1])
        pass_a(s, phase, 0, NX, xy_recv.at[phase, 3], to_y)

        @pl.when(phase < 2)
        def _():
            part = 2 * phase
            forward_b(part + 1)

        pass_a(row_of(xm, y, b), phase, 0, 4, core_recv.at[phase, 1], to_b)
        pass_a(row_of(xp, y, b), phase, 0, 4, core_recv.at[phase, 2], to_b)
        for index in range(2):
            s = row_of(x2, (y, y1)[index], b)
            got_a(s, phase, NX, hy, yx2_recv.at[phase, index, 0])
            got_a(s, phase, NX + hy, ny - hy, yx2_recv.at[phase, index, 1])
        pass_a(row_of(x2, y, b), phase, 0, 4, core_recv.at[phase, 3], to_b)
        for index, xx in enumerate((x, xm, xp, x2)):
            s = row_of(xx, y1, b)
            got_a(s, phase, 0, NX, xy_recv.at[phase, index])
            pass_a(s, phase, 0, 4, core_recv.at[phase, 4 + index], to_b)

        @pl.when(phase < 2)
        def _():
            part = 2 * phase
            last_b(part)
            last_b(part + 1)

        for index, (xx, yy) in enumerate(
            ((x, y), (xm, y), (xp, y), (x2, y), (x, y1), (xm, y1), (xp, y1), (x2, y1))
        ):
            got_a(row_of(xx, yy, b1), phase, 0, 4, core_recv.at[phase, index])

        total[...] = jnp.zeros_like(total)

        def source_step(source, inner):
            multiply(source, phase)
            return inner

        lax.fori_loop(0, 16, source_step, 0)

        w = third(phase)

        def swap(first_mine, count, row_mine):
            def one(n, inner):
                mine[first_mine + n] = total[row_mine + n].astype(jnp.bfloat16)
                return inner

            lax.fori_loop(0, count, one, 0)

        def give(first, count, row, index):
            def one(n, inner):
                outgoing_part[first + n] = total[row + n].astype(jnp.bfloat16)
                return inner

            lax.fori_loop(0, count, one, 0)
            remote(
                outgoing_part.at[pl.ds(first, count)],
                incoming_part.at[pl.ds(first, count)],
                p_send.at[index],
                p_recv.at[index],
                to_l,
            ).start()

        @pl.when((w == 0) & (l == 0))
        def _():
            swap(0, 8, 0)

        @pl.when((w == 0) & (l == 1))
        def _():
            give(0, 8, 0, 0)

        @pl.when((w == 2) & (l == 1))
        def _():
            swap(4, 8, 0)

        @pl.when((w == 2) & (l == 0))
        def _():
            give(4, 8, 0, 0)

        @pl.when((w == 1) & (l == 0))
        def _():
            give(0, 4, 4, 1)
            swap(8, 4, 0)

        @pl.when((w == 1) & (l == 1))
        def _():
            give(8, 4, 0, 1)
            swap(0, 4, 4)

        return carry

    lax.fori_loop(0, PHASES, run_phase, 0)

    def part_copy(first, count, index):
        return remote(
            outgoing_part.at[pl.ds(first, count)],
            incoming_part.at[pl.ds(first, count)],
            p_send.at[index],
            p_recv.at[index],
            to_l,
        )

    @pl.when(l == 0)
    def _():
        part_copy(0, 8, 0).wait_recv()
        part_copy(8, 4, 1).wait_recv()

    @pl.when(l == 1)
    def _():
        part_copy(4, 8, 0).wait_recv()
        part_copy(0, 4, 1).wait_recv()

    def fill(owner):
        def one(n, inner):
            index = slot_source[owner * 6 + n]
            value = mine[index].astype(jnp.float32) + incoming_part[index].astype(jnp.float32)
            slots[owner, n] = (value * slot_used[owner * 6 + n].astype(jnp.float32)).astype(jnp.bfloat16)
            return inner

        lax.fori_loop(0, 6, one, 0)

    def slot_copy(owner, index, device):
        return remote(slots.at[owner], out_ref.at[c], o_send.at[index], o_recv.at[index], device)

    for index, (owner, device) in enumerate(((z2, to_z2), (zp, to_zp), (zm, to_zm))):
        fill(owner)
        slot_copy(owner, index, device).start()
    fill(c)
    stay = pltpu.make_async_copy(slots.at[c], out_ref.at[c], local_sem.at[PHASES + 4])
    stay.start()
    for phase in range(PHASES):
        ref = abuf.at[pl.ds(0, 5)]
        remote(ref, ref, a_send.at[phase], core_recv.at[phase, 0], to_b).wait_send()
    for part in range(4):
        ref = bbuf.at[pl.ds(0, 3), part]
        remote(ref, ref, b_send.at[part], bz_recv.at[part, 0], to_zp).wait_send()

    @pl.when(l == 0)
    def _():
        part_copy(4, 8, 0).wait_send()
        part_copy(0, 4, 1).wait_send()

    @pl.when(l == 1)
    def _():
        part_copy(0, 8, 0).wait_send()
        part_copy(8, 4, 1).wait_send()

    stay.wait()
    for index, (owner, device, sender) in enumerate(((z2, to_z2, z2), (zp, to_zp, zm), (zm, to_zm, zp))):
        slot_copy(owner, index, device).wait_send()
        remote(slots.at[owner], out_ref.at[sender], o_send.at[index], o_recv.at[index], device).wait_recv()


def on_device(a_blocks, b_blocks, a_offsets, b_offsets, keep_offsets, owners):
    a_part = a_blocks.reshape(12, BLOCK, BLOCK)
    b_part = b_blocks.reshape(4, 8, BLOCK, BLOCK)
    a_mask = jnp.sum(1 << (a_offsets[:, 0, :] + 8), axis=1)
    b_mask = jnp.sum(1 << (b_offsets + 8), axis=1)
    keep = keep_offsets[:, 0, 0]
    owner = owners[:, 0, 0]
    names = jnp.arange(4, dtype=jnp.int32)
    same = (owner[:, None] == owner[None, :]) & (jnp.arange(12)[:, None] > jnp.arange(12)[None, :])
    rank = jnp.sum(same.astype(jnp.int32), axis=1)
    chosen = (owner[None, None, :] == names[:, None, None]) & (
        rank[None, None, :] == jnp.arange(6, dtype=jnp.int32)[None, :, None]
    )
    slot_source = jnp.sum(chosen * jnp.arange(12, dtype=jnp.int32), axis=2).reshape(24)
    slot_used = jnp.sum(chosen.astype(jnp.int32), axis=2).reshape(24)
    smem = pl.BlockSpec(memory_space=pltpu.SMEM)
    anywhere = pl.BlockSpec(memory_space=pl.ANY)
    dma = pltpu.SemaphoreType.DMA
    block = (BLOCK, BLOCK)
    arrived = pl.pallas_call(
        kernel,
        out_shape=jax.ShapeDtypeStruct((4, 6, BLOCK, BLOCK), jnp.bfloat16),
        in_specs=[anywhere, anywhere, smem, smem, smem, smem, smem],
        out_specs=anywhere,
        scratch_shapes=[
            pltpu.VMEM((16, 12) + block, jnp.bfloat16),
            pltpu.VMEM((4, 4, 4) + block, jnp.bfloat16),
            pltpu.VMEM((8,) + block, jnp.float32),
            pltpu.VMEM((12,) + block, jnp.bfloat16),
            pltpu.VMEM((12,) + block, jnp.bfloat16),
            pltpu.VMEM((12,) + block, jnp.bfloat16),
            pltpu.VMEM((4, 6) + block, jnp.bfloat16),
            dma((PHASES + 5,)),
            dma((PHASES,)),
            dma((4,)),
            dma((2,)),
            dma((3,)),
            dma((PHASES, 2)),
            dma((PHASES, 2)),
            dma((PHASES, 4)),
            dma((PHASES,)),
            dma((PHASES, 2, 2)),
            dma((PHASES, 2, 2)),
            dma((PHASES, 8)),
            dma((4, 2)),
            dma((4, 2)),
            dma((2,)),
            dma((3,)),
        ],
        compiler_params=pltpu.CompilerParams(
            collective_id=0, has_side_effects=True, vmem_limit_bytes=56 << 20
        ),
        cost_estimate=pl.CostEstimate(
            flops=192 * 2 * BLOCK**3, bytes_accessed=10 << 20, transcendentals=0
        ),
        name="banded_product",
    )(a_part, b_part, a_mask, b_mask, keep, slot_source, slot_used)
    return arrived.reshape(1, 1, 1, 4, 6, BLOCK, BLOCK)


def solution(mesh):
    return jax.shard_map(
        on_device,
        mesh=mesh,
        in_specs=(
            P("row", "col", "layer", None, None, None),
            P("row", "col", "layer", None, None, None),
            P(None, "col", None),
            P(),
            P(None, "col", "row"),
            P("layer", "col", "row"),
        ),
        out_specs=P("row", "col", "layer", None, None, None, None),
        check_vma=False,
    )
```

time: 616 us -> 219 us (0.36)
  matrix products: 212 us -> 0 us
  Pallas kernels: 0 us -> 207 us
  local copies, waits for them, and re-layouts: 153 us -> 5.33 us
  other arithmetic: 123 us -> 4.36 us
  waiting for transfers between devices: 46.3 us -> 0 us
  blocking collectives: 41.8 us -> 0 us
  starting transfers between devices: 18.3 us -> 0 us
  between operations: 14.1 us -> 0.02 us
    dot_general x49 -> x0, matrix products: 212 us -> none  [the longest x16 115 us: add_piece(): jnp.einsum('wgab,wgu->wuab', products, placing, precision=lax.Precision.H...]
    pallas_call x0 -> x1, Pallas kernels: none -> 207 us  [on_device(): pl.pallas_call(kernel, out_shape=jax.ShapeDtypeStruct((4, 6, BLOCK, BLOCK...]
    add x29 -> x0, other arithmetic: 93.7 us -> none  [the longest x15 92.7 us: add_piece(): return total + added.reshape(group_rows, block_size, block_size)]
    reduce_scatter x1 -> x0, waiting for transfers between devices: 46.2 us -> none  [on_device(): lax.psum_scatter(total.astype(jnp.bfloat16), 'layer', scatter_dimension=0...]
    all_to_all x1 -> x0, blocking collectives: 41.8 us -> none  [on_device(): lax.all_to_all(outgoing, 'col', split_axis=0, concat_axis=0, tiled=True)]
    reshape x12 -> x2, local copies, waits for them, and re-layouts: 39.2 us -> 1.28 us  [the longest x1 0.68 us: on_device(): slot_used = jnp.sum(chosen.astype(jnp.int32), axis=2).reshape(24)]
    dot_general x16 -> x0, local copies, waits for them, and re-layouts: 34.9 us -> none  [add_piece(): jnp.einsum('wgab,wgu->wuab', products, placing, precision=lax.Precision.H...]
    while x12 -> x0, local copies, waits for them, and re-layouts: 32.2 us -> none
  transfers between devices with their start and end apart: 19 -> 0, of which waited for: 1 -> 0; matrix products, arithmetic and copies ran while one was open for 74% -> 0% of each run, Pallas kernels for 0% -> 0%
where the time goes in v1:
time: 219 us; the launch traced here: 216 us
  Pallas kernels  207 us (95%)
  local copies, waits for them, and re-layouts  5.33 us (2%)
  other arithmetic  4.36 us (2%)
    pallas_call x1, Pallas kernels, on_device(): pl.pallas_call(kernel, out_shape=jax.ShapeDtypeStruct((4, 6, BLOCK, BLOCK...  207 us

profile of v1, /device:TPU:8, one launch (start us, length us, event | category | flops | bytes accessed | tf_op | source)
XLA Modules:
  0.0 216.2 jit_solution(12434266443394191654)
XLA Ops:
  0.0 1.2 shift-left_reduce_fusion.1.a_mask
  1.2 0.9 convert_reduce_fusion
  2.1 0.7 iota_compare_fusion.2
  2.8 1.3 shift-left_reduce_fusion.b_mask
  4.1 0.3 fusion.1
  4.4 0.1 copy.8
  4.5 0.7 reshape.73.slot_used
  5.1 0.1 copy.7
  5.2 0.6 reshape.72.slot_source
  5.8 206.5 %banded_product.1 = bf16[4,6,256,256]{3,2,1,0:T(8,128)(2,1)} custom-call(bf16[12,256,256]{2,1,0:T(8,128)(2,1)} %bitcast.7, bf16[4,8,256,256]{3,2,1,0:T(8,128)(2,1)} %bitcast.6, s32[24]{0:T(128)} %shift-left_reduce_fusion.1.a_mask, s32[256]{0:T(256)} %shift-left_reduce_fusion.b_mask, s32[24]{0:T(128)} %bitcast.10, s32[24]{0:T(128)} %reshape.72.slot_source, ...), custom_call_target="tpu_custom_call" | custom-call | flops 6442450944 | bytes 10485760 | tf_op jit(solution)/shard_map/banded_product/pallas_call | solution.py:380
  212.4 3.9 %copy.10 = bf16[1,1,1,4,6,256,256]{6,5,4,3,2,1,0:T(8,128)(2,1)} copy(bf16[1,1,1,4,6,256,256]{6,5,4,3,2,1,0:T(8,128)(2,1)} %bitcast.5) | data formatting | bytes 6291456
  (1 shorter events, 0.0 us)

commit v2 on v1

--- a/solution.py
+++ b/solution.py
@@ -10,7 +10,8 @@
 MESH = pl.DeviceIdType.MESH
 BLOCK = 256
 PHASES = 3
-NX = 2
+NX = 1
+NY = 3
 
 
 def mod(value, count):
@@ -49,6 +50,8 @@
     bz2_recv,
     p_recv,
     o_recv,
+    edge_send,
+    edge_recv,
 ):
     r = lax.axis_index("row")
     c = lax.axis_index("col")
@@ -77,7 +80,7 @@
         )
 
     def third(phase):
-        return lax.rem(2 * phase, jnp.int32(3))
+        return jnp.where(phase == 0, 2 * l1, jnp.where(phase == 1, 2 * l, 1))
 
     def blocks(source, phase, first, count):
         return abuf.at[source, pl.ds(third(phase) * 4 + first, count)]
@@ -89,10 +92,6 @@
     def got_a(source, phase, first, count, recv):
         ref = blocks(source, phase, first, count)
         remote(ref, ref, a_send.at[phase], recv, to_b).wait_recv()
-
-    ny = 4 - NX
-    half = NX // 2
-    hy = ny // 2
 
     def own_copy(phase):
         return pltpu.make_async_copy(
@@ -106,13 +105,12 @@
 
     def send_own(phase):
         own_copy(phase).wait()
-        pass_a(r, phase, NX, ny, yy_recv.at[phase], to_y)
+        pass_a(r, phase, NX, NY, yy_recv.at[phase], to_y)
         pass_a(r, phase, 0, NX, x_recv.at[phase, 0], to_xp)
         pass_a(r, phase, 0, NX, x_recv.at[phase, 1], to_xm)
-        pass_a(r, phase, NX, ny, yx_recv.at[phase, 0, 0], to_xp)
-        pass_a(r, phase, NX, ny, yx_recv.at[phase, 0, 1], to_xm)
+        pass_a(r, phase, NX, NY, yx_recv.at[phase, 0, 0], to_xp)
+        pass_a(r, phase, NX, NY, yx_recv.at[phase, 0, 1], to_xm)
         pass_a(r, phase, 0, NX, xy_recv.at[phase, 0], to_y)
-        pass_a(r, phase, 0, 4, core_recv.at[phase, 0], to_b)
 
     def pass_b(source, part, first, count, recv, device):
         ref = bbuf.at[source, part, pl.ds(first, count)]
@@ -136,6 +134,60 @@
     def last_b(part):
         got_b(z2, part, 0, 2, bz2_recv.at[part, 0])
         got_b(z2, part, 2, 2, bz2_recv.at[part, 1])
+
+    edge = 3 * l1
+    middle = 2 - l
+
+    def inside(source, n):
+        q = mod(r + 4 * source + n, 16)
+        return jnp.where(l == 0, jnp.where(q <= 6, 1, 0), jnp.where(q >= 8, 1, 0)) == 1
+
+    def edge_copy(source, n, send, recv, device):
+        ref = bbuf.at[source, edge, n]
+        return remote(ref, ref, edge_send.at[send, n], edge_recv.at[recv, n], device)
+
+    def send_own_edge():
+        b_own_copy(edge).wait()
+        for n in range(4):
+
+            @pl.when(inside(c, n))
+            def _():
+                edge_copy(c, n, 0, 0, to_zp).start()
+                edge_copy(c, n, 1, 1, to_zm).start()
+
+    def forward_edge():
+        for n in range(4):
+
+            @pl.when(inside(zm, n))
+            def _():
+                edge_copy(zm, n, 0, 0, to_zp).wait_recv()
+                if n < 2:
+                    edge_copy(zm, n, 2, 2, to_zp).start()
+
+            @pl.when(inside(zp, n))
+            def _():
+                edge_copy(zp, n, 1, 1, to_zm).wait_recv()
+                if n >= 2:
+                    edge_copy(zp, n, 2, 2, to_zm).start()
+
+    def last_edge():
+        for n in range(4):
+
+            @pl.when(inside(z2, n))
+            def _():
+                edge_copy(z2, n, 2, 2, to_zp).wait_recv()
+
+    def sent_edge():
+        for n in range(4):
+
+            @pl.when(inside(c, n))
+            def _():
+                edge_copy(c, n, 0, 0, to_zp).wait_send()
+                edge_copy(c, n, 1, 1, to_zm).wait_send()
+
+            @pl.when(inside(zm if n < 2 else zp, n))
+            def _():
+                edge_copy(c, n, 2, 2, to_zp).wait_send()
 
     def multiply(source, phase):
         piece = 16 * l + mod(source + 4 * c, 16)
@@ -160,96 +212,117 @@
             )
             total[u] += product * weight
 
-    for phase in range(PHASES):
-        own_copy(phase).start()
-    for part in range(4):
-        b_own_copy(part).start()
+    own_copy(0).start()
+    b_own_copy(edge).start()
+    b_own_copy(middle).start()
+    own_copy(1).start()
+    b_own_copy(2 * l).start()
+    b_own_copy(2 * l + 1).start()
+    own_copy(2).start()
     send_own(0)
-    send_own_b(0)
-    send_own_b(1)
-
-    def run_phase(phase, carry):
+    send_own_b(middle)
+    send_own_edge()
+    pass_a(r, 0, 0, 4, core_recv.at[0, 0], to_b)
+    send_own(1)
+
+    def send_on(phase):
         s = row_of(x, y1, b)
-        got_a(s, phase, NX, ny, yy_recv.at[phase])
-        pass_a(s, phase, NX, ny, yx_recv.at[phase, 1, 0], to_xp)
-        pass_a(s, phase, NX, ny, yx_recv.at[phase, 1, 1], to_xm)
-
-        @pl.when(phase < 2)
-        def _():
-            part = 2 * phase
-            forward_b(part)
+        got_a(s, phase, NX, NY, yy_recv.at[phase])
+        pass_a(s, phase, NX, NY, yx_recv.at[phase, 1, 0], to_xp)
+        pass_a(s, phase, NX, NY, yx_recv.at[phase, 1, 1], to_xm)
+
+        s = row_of(xp, y, b)
+        got_a(s, phase, 0, NX, x_recv.at[phase, 1])
+        pass_a(s, phase, 0, NX, xy_recv.at[phase, 1], to_y)
+
+        @pl.when(b == 1)
+        def _():
+            pass_a(row_of(xp, y, b), phase, 0, NX, x2_recv.at[phase], to_xm)
 
         s = row_of(xm, y, b)
         got_a(s, phase, 0, NX, x_recv.at[phase, 0])
-        pass_a(s, phase, 0, half, x2_recv.at[phase, 0], to_xp)
-        pass_a(s, phase, 0, NX, xy_recv.at[phase, 1], to_y)
-        s = row_of(xp, y, b)
-        got_a(s, phase, 0, NX, x_recv.at[phase, 1])
-        pass_a(s, phase, half, NX - half, x2_recv.at[phase, 1], to_xm)
+        pass_a(s, phase, 0, NX, xy_recv.at[phase, 3], to_y)
+
+        @pl.when(b == 0)
+        def _():
+            pass_a(row_of(xm, y, b), phase, 0, NX, x2_recv.at[phase], to_xp)
+
+        for index, yy in ((0, y), (1, y1)):
+            split = 1 + index
+            s = row_of(xm, yy, b)
+            got_a(s, phase, NX, NY, yx_recv.at[phase, index, 0])
+            pass_a(s, phase, NX, split, yx2_recv.at[phase, index, 0], to_xp)
+            s = row_of(xp, yy, b)
+            got_a(s, phase, NX, NY, yx_recv.at[phase, index, 1])
+            pass_a(s, phase, NX + split, NY - split, yx2_recv.at[phase, index, 1], to_xm)
+
+        s = row_of(x2, y, b)
+        got_a(s, phase, 0, NX, x2_recv.at[phase])
         pass_a(s, phase, 0, NX, xy_recv.at[phase, 2], to_y)
-        for index, yy in ((0, y), (1, y1)):
-            s = row_of(xm, yy, b)
-            got_a(s, phase, NX, ny, yx_recv.at[phase, index, 0])
-            pass_a(s, phase, NX, hy, yx2_recv.at[phase, index, 0], to_xp)
-            s = row_of(xp, yy, b)
-            got_a(s, phase, NX, ny, yx_recv.at[phase, index, 1])
-            pass_a(s, phase, NX + hy, ny - hy, yx2_recv.at[phase, index, 1], to_xm)
-
+        for n in (1, 3):
+            pass_a(row_of(mod(x + n, 4), y, b), phase, 0, 4, core_recv.at[phase, n], to_b)
+
+    send_on(0)
+    send_own(2)
+    forward_b(middle)
+    forward_edge()
+    send_own_b(2 * l)
+    send_own_b(2 * l + 1)
+
+    def run_phase(phase, carry):
         @pl.when(phase < 2)
         def _():
-            send_own(phase + 1)
-
-        @pl.when(phase < 1)
-        def _():
-            send_own_b(2)
-            send_own_b(3)
-
-        s = row_of(x2, y, b)
-        got_a(s, phase, 0, half, x2_recv.at[phase, 0])
-        got_a(s, phase, half, NX - half, x2_recv.at[phase, 1])
-        pass_a(s, phase, 0, NX, xy_recv.at[phase, 3], to_y)
+            send_on(phase + 1)
+
+        @pl.when(phase == 1)
+        def _():
+            forward_b(2 * l)
+            forward_b(2 * l + 1)
+
+        for index in range(2):
+            split = 1 + index
+            s = row_of(x2, (y, y1)[index], b)
+            got_a(s, phase, NX, split, yx2_recv.at[phase, index, 0])
+            got_a(s, phase, NX + split, NY - split, yx2_recv.at[phase, index, 1])
+        pass_a(row_of(x2, y, b), phase, 0, 4, core_recv.at[phase, 2], to_b)
+        for n in (0, 1, 3, 2):
+            s = row_of(mod(x + n, 4), y1, b)
+            got_a(s, phase, 0, NX, xy_recv.at[phase, n])
+            pass_a(s, phase, 0, 4, core_recv.at[phase, 4 + n], to_b)
+
+        @pl.when(phase == 0)
+        def _():
+            last_b(middle)
+            last_edge()
+
+        @pl.when(phase == 1)
+        def _():
+            last_b(2 * l)
+            last_b(2 * l + 1)
 
         @pl.when(phase < 2)
         def _():
-            part = 2 * phase
-            forward_b(part + 1)
-
-        pass_a(row_of(xm, y, b), phase, 0, 4, core_recv.at[phase, 1], to_b)
-        pass_a(row_of(xp, y, b), phase, 0, 4, core_recv.at[phase, 2], to_b)
-        for index in range(2):
-            s = row_of(x2, (y, y1)[index], b)
-            got_a(s, phase, NX, hy, yx2_recv.at[phase, index, 0])
-            got_a(s, phase, NX + hy, ny - hy, yx2_recv.at[phase, index, 1])
-        pass_a(row_of(x2, y, b), phase, 0, 4, core_recv.at[phase, 3], to_b)
-        for index, xx in enumerate((x, xm, xp, x2)):
-            s = row_of(xx, y1, b)
-            got_a(s, phase, 0, NX, xy_recv.at[phase, index])
-            pass_a(s, phase, 0, 4, core_recv.at[phase, 4 + index], to_b)
-
-        @pl.when(phase < 2)
-        def _():
-            part = 2 * phase
-            last_b(part)
-            last_b(part + 1)
-
-        for index, (xx, yy) in enumerate(
-            ((x, y), (xm, y), (xp, y), (x2, y), (x, y1), (xm, y1), (xp, y1), (x2, y1))
-        ):
-            got_a(row_of(xx, yy, b1), phase, 0, 4, core_recv.at[phase, index])
+            pass_a(r, phase + 1, 0, 4, core_recv.at[phase + 1, 0], to_b)
 
         total[...] = jnp.zeros_like(total)
 
-        def source_step(source, inner):
+        def of_this_core(n, inner):
+            multiply(row_of(mod(x + n, 4), mod(y + n // 4, 2), b), phase)
+            return inner
+
+        lax.fori_loop(0, 8, of_this_core, 0)
+
+        def of_sibling(n, inner):
+            source = row_of(mod(x + n, 4), mod(y + n // 4, 2), b1)
+            got_a(source, phase, 0, 4, core_recv.at[phase, n])
             multiply(source, phase)
             return inner
 
-        lax.fori_loop(0, 16, source_step, 0)
-
-        w = third(phase)
-
-        def swap(first_mine, count, row_mine):
+        lax.fori_loop(0, 8, of_sibling, 0)
+
+        def stay_here(first, count, row):
             def one(n, inner):
-                mine[first_mine + n] = total[row_mine + n].astype(jnp.bfloat16)
+                mine[first + n] = total[row + n].astype(jnp.bfloat16)
                 return inner
 
             lax.fori_loop(0, count, one, 0)
@@ -260,43 +333,22 @@
                 return inner
 
             lax.fori_loop(0, count, one, 0)
-            remote(
-                outgoing_part.at[pl.ds(first, count)],
-                incoming_part.at[pl.ds(first, count)],
-                p_send.at[index],
-                p_recv.at[index],
-                to_l,
-            ).start()
-
-        @pl.when((w == 0) & (l == 0))
-        def _():
-            swap(0, 8, 0)
-
-        @pl.when((w == 0) & (l == 1))
-        def _():
-            give(0, 8, 0, 0)
-
-        @pl.when((w == 2) & (l == 1))
-        def _():
-            swap(4, 8, 0)
-
-        @pl.when((w == 2) & (l == 0))
-        def _():
-            give(4, 8, 0, 0)
-
-        @pl.when((w == 1) & (l == 0))
-        def _():
-            give(0, 4, 4, 1)
-            swap(8, 4, 0)
-
-        @pl.when((w == 1) & (l == 1))
-        def _():
-            give(8, 4, 0, 1)
-            swap(0, 4, 4)
+            part_copy(first, count, index).start()
+
+        @pl.when(phase == 0)
+        def _():
+            give(4 * l1, 8, 0, 0)
+
+        @pl.when(phase == 1)
+        def _():
+            stay_here(4 * l, 8, 0)
+
+        @pl.when(phase == 2)
+        def _():
+            give(8 * l, 4, 4 * l1, 1)
+            stay_here(8 * l1, 4, 4 * l)
 
         return carry
-
-    lax.fori_loop(0, PHASES, run_phase, 0)
 
     def part_copy(first, count, index):
         return remote(
@@ -307,15 +359,10 @@
             to_l,
         )
 
-    @pl.when(l == 0)
-    def _():
-        part_copy(0, 8, 0).wait_recv()
-        part_copy(8, 4, 1).wait_recv()
-
-    @pl.when(l == 1)
-    def _():
-        part_copy(4, 8, 0).wait_recv()
-        part_copy(0, 4, 1).wait_recv()
+    lax.fori_loop(0, PHASES, run_phase, 0)
+
+    part_copy(4 * l, 8, 0).wait_recv()
+    part_copy(8 * l1, 4, 1).wait_recv()
 
     def fill(owner):
         def one(n, inner):
@@ -338,20 +385,12 @@
     for phase in range(PHASES):
         ref = abuf.at[pl.ds(0, 5)]
         remote(ref, ref, a_send.at[phase], core_recv.at[phase, 0], to_b).wait_send()
-    for part in range(4):
+    for part in (middle, 2 * l, 2 * l + 1):
         ref = bbuf.at[pl.ds(0, 3), part]
         remote(ref, ref, b_send.at[part], bz_recv.at[part, 0], to_zp).wait_send()
-
-    @pl.when(l == 0)
-    def _():
-        part_copy(4, 8, 0).wait_send()
-        part_copy(0, 4, 1).wait_send()
-
-    @pl.when(l == 1)
-    def _():
-        part_copy(0, 8, 0).wait_send()
-        part_copy(8, 4, 1).wait_send()
-
+    sent_edge()
+    part_copy(4 * l1, 8, 0).wait_send()
+    part_copy(8 * l, 4, 1).wait_send()
     stay.wait()
     for index, (owner, device, sender) in enumerate(((z2, to_z2, z2), (zp, to_zp, zm), (zm, to_zm, zp))):
         slot_copy(owner, index, device).wait_send()
@@ -396,7 +435,7 @@
             dma((2,)),
             dma((3,)),
             dma((PHASES, 2)),
-            dma((PHASES, 2)),
+            dma((PHASES,)),
             dma((PHASES, 4)),
             dma((PHASES,)),
             dma((PHASES, 2, 2)),
@@ -406,6 +445,8 @@
             dma((4, 2)),
             dma((2,)),
             dma((3,)),
+            dma((3, 4)),
+            dma((3, 4)),
         ],
         compiler_params=pltpu.CompilerParams(
             collective_id=0, has_side_effects=True, vmem_limit_bytes=56 << 20

time: 219 us -> 184 us (0.84)
  Pallas kernels: 207 us -> 172 us
    pallas_call x1, Pallas kernels: 207 us -> 172 us  [on_device(): pl.pallas_call(kernel, out_shape=jax.ShapeDtypeStruct((4, 6, BLOCK, BLOCK...]
where the time goes in v2:
time: 184 us; the launch traced here: 182 us
  Pallas kernels  172 us (93%)
  local copies, waits for them, and re-layouts  5.33 us (3%)
  other arithmetic  4.36 us (2%)
    pallas_call x1, Pallas kernels, on_device(): pl.pallas_call(kernel, out_shape=jax.ShapeDtypeStruct((4, 6, BLOCK, BLOCK...  172 us
    unnamed x1, local copies, waits for them, and re-layouts  3.86 us

profile of v2, /device:TPU:8, one launch (start us, length us, event | category | flops | bytes accessed | tf_op | source)
XLA Modules:
  0.0 181.7 jit_solution(12502723806455790175)
XLA Ops:
  0.0 1.2 shift-left_reduce_fusion.1.a_mask
  1.2 0.9 convert_reduce_fusion
  2.1 0.7 iota_compare_fusion.2
  2.8 1.3 shift-left_reduce_fusion.b_mask
  4.1 0.3 fusion.1
  4.4 0.1 copy.8
  4.5 0.7 reshape.73.slot_used
  5.1 0.1 copy.7
  5.2 0.6 reshape.72.slot_source
  5.8 172.0 %banded_product.1 = bf16[4,6,256,256]{3,2,1,0:T(8,128)(2,1)} custom-call(bf16[12,256,256]{2,1,0:T(8,128)(2,1)} %bitcast.7, bf16[4,8,256,256]{3,2,1,0:T(8,128)(2,1)} %bitcast.6, s32[24]{0:T(128)} %shift-left_reduce_fusion.1.a_mask, s32[256]{0:T(256)} %shift-left_reduce_fusion.b_mask, s32[24]{0:T(128)} %bitcast.10, s32[24]{0:T(128)} %reshape.72.slot_source, ...), custom_call_target="tpu_custom_call" | custom-call | flops 6442450944 | bytes 10485760 | tf_op jit(solution)/shard_map/banded_product/pallas_call | solution.py:419
  177.8 3.9 %copy.10 = bf16[1,1,1,4,6,256,256]{6,5,4,3,2,1,0:T(8,128)(2,1)} copy(bf16[1,1,1,4,6,256,256]{6,5,4,3,2,1,0:T(8,128)(2,1)} %bitcast.5) | data formatting | bytes 6291456
  (1 shorter events, 0.0 us)

commit v3 on v1

v3 whole, which is shorter than its diff:
```python
import functools

import jax
import jax.numpy as jnp
from jax import lax
from jax.experimental import pallas as pl
from jax.experimental.pallas import tpu as pltpu
from jax.sharding import PartitionSpec as P

MESH = pl.DeviceIdType.MESH
BLOCK = 256


def mod(value, count):
    return lax.rem(value + 32 * count, jnp.int32(count))


def kernel(
    a_ref,
    b_ref,
    a_offsets,
    b_offsets,
    keep,
    owners,
    keep_vector,
    out_ref,
    abuf,
    bbuf,
    total,
    parts,
    leaving,
    swapped,
    slots,
    keep_arrived,
    keep_other,
    a_mask,
    b_mask,
    rank,
    slot_source,
    slot_used,
    local_sem,
    keep_sem,
    a_send,
    yy_recv,
    yx_recv,
    yx2_recv,
    core_recv,
    by_send,
    by_recv,
    bz_send,
    bz_recv,
    p_send,
    p_recv,
    o_send,
    o_recv,
):
    r = lax.axis_index("row")
    c = lax.axis_index("col")
    l = lax.axis_index("layer")
    x, y, b = r // 4, (r // 2) % 2, r % 2

    def row_of(xx, yy, bb):
        return xx * 4 + yy * 2 + bb

    xp, xm, x2 = mod(x + 1, 4), mod(x - 1, 4), mod(x + 2, 4)
    zp, zm, z2 = mod(c + 1, 4), mod(c - 1, 4), mod(c + 2, 4)
    y1, b1, l1 = 1 - y, 1 - b, 1 - l
    r1 = row_of(x, y1, b)
    to_xp, to_xm = {"row": row_of(xp, y, b)}, {"row": row_of(xm, y, b)}
    to_y, to_b = {"row": r1}, {"row": row_of(x, y, b1)}
    to_zp, to_zm, to_z2 = {"col": zp}, {"col": zm}, {"col": z2}
    to_l, to_yl = {"layer": l1}, {"row": r1, "layer": l1}

    barrier = pltpu.get_barrier_semaphore()
    for device in (to_xp, to_xm, to_y, to_b, to_zp, to_zm, to_z2, to_l, to_yl):
        pl.semaphore_signal(barrier, inc=1, device_id=device, device_id_type=MESH)
    pl.semaphore_wait(barrier, 9)

    def remote(src, dst, send, recv, device):
        return pltpu.make_async_remote_copy(
            src_ref=src, dst_ref=dst, send_sem=send, recv_sem=recv, device_id=device, device_id_type=MESH
        )

    def third(phase):
        return 2 * y if phase == 0 else 1

    def pass_a(source, phase, first, count, recv, device):
        ref = abuf.at[phase, source, pl.ds(first, count)]
        remote(ref, ref, a_send.at[phase], recv, device).start()

    def got_a(source, phase, first, count, recv):
        ref = abuf.at[phase, source, pl.ds(first, count)]
        remote(ref, ref, a_send.at[phase], recv, to_b).wait_recv()

    def own_copy(phase):
        return pltpu.make_async_copy(
            a_ref.at[pl.ds(third(phase) * 4, 4)], abuf.at[phase, r], local_sem.at[phase]
        )

    def a_to_y(phase):
        first = 8 * y1 if phase == 0 else 4
        remote(
            a_ref.at[pl.ds(first, 4)], abuf.at[phase, r], a_send.at[phase], yy_recv.at[phase], to_y
        ).start()

    def a_along_x(phase, yy):
        index = 0 if yy is y else 1
        s = row_of(x, yy, b)
        pass_a(s, phase, 0, 4, yx_recv.at[phase, index, 0], to_xp)
        pass_a(s, phase, 0, 4, yx_recv.at[phase, index, 1], to_xm)

    def a_further(phase, yy):
        index = 0 if yy is y else 1
        s = row_of(xm, yy, b)
        got_a(s, phase, 0, 4, yx_recv.at[phase, index, 0])
        pass_a(s, phase, 0, 2, yx2_recv.at[phase, index, 0], to_xp)
        s = row_of(xp, yy, b)
        got_a(s, phase, 0, 4, yx_recv.at[phase, index, 1])
        pass_a(s, phase, 2, 2, yx2_recv.at[phase, index, 1], to_xm)

    def to_sibling(phase, n):
        source = row_of(mod(x + n, 4), mod(y + n // 4, 2), b)
        pass_a(source, phase, 0, 4, core_recv.at[phase, n], to_b)

    def a_last(phase, yy):
        index = 0 if yy is y else 1
        s = row_of(x2, yy, b)
        got_a(s, phase, 0, 2, yx2_recv.at[phase, index, 0])
        got_a(s, phase, 2, 2, yx2_recv.at[phase, index, 1])

    other_full, other_edge = 3 + l, 4 - l
    own_second, own_last = 2 * y, 2 - 2 * y

    def b_own_copy(part):
        return pltpu.make_async_copy(
            b_ref.at[:, mod(y + part - l, 8)], bbuf.at[part, c], local_sem.at[2 + part]
        )

    def b_full_over_y():
        return remote(
            b_ref.at[:, mod(2 * y1, 8)], bbuf.at[other_full, c], by_send.at[4], by_recv.at[4], to_y
        )

    def b_edge_over_y(n):
        return remote(
            b_ref.at[n, mod(2 * y1 + 1 - 2 * l, 8)],
            bbuf.at[other_edge, c, n],
            by_send.at[n],
            by_recv.at[n],
            to_y,
        )

    def near(column, source, n):
        q = mod(column + 4 * source + n, 16)
        return jnp.where(l == 0, jnp.where(q <= 6, 1, 0), jnp.where(q >= 8, 1, 0))

    def edges_over_y(column, act):
        for n in range(4):

            @pl.when(near(column, c, n) == 1)
            def _():
                act(b_edge_over_y(n))

    def inside(part, source, n):
        column = jnp.where(part >= 3, r1, r)
        whole = jnp.where(part >= 3, jnp.where(part == other_full, 1, 0), jnp.where(part == 2 * l1, 0, 1))
        return whole + near(column, source, n) > 0

    def b_copy(part, source, n, way, device):
        ref = bbuf.at[part, source, n]
        return remote(ref, ref, bz_send.at[way, part, n], bz_recv.at[way, part, n], device)

    def b_start(part):
        for n in range(4):

            @pl.when(inside(part, c, n))
            def _():
                b_copy(part, c, n, 0, to_zp).start()
                b_copy(part, c, n, 1, to_zm).start()

    def b_further(part):
        for n in range(4):

            @pl.when(inside(part, zm, n))
            def _():
                b_copy(part, zm, n, 0, to_zp).wait_recv()
                if n < 2:
                    b_copy(part, zm, n, 2, to_zp).start()

            @pl.when(inside(part, zp, n))
            def _():
                b_copy(part, zp, n, 1, to_zm).wait_recv()
                if n >= 2:
                    b_copy(part, zp, n, 2, to_zm).start()

    def b_last(part):
        for n in range(4):

            @pl.when(inside(part, z2, n))
            def _():
                b_copy(part, z2, n, 2, to_zp).wait_recv()

    def b_sent(part):
        for n in range(4):

            @pl.when(inside(part, c, n))
            def _():
                b_copy(part, c, n, 0, to_zp).wait_send()
                b_copy(part, c, n, 1, to_zm).wait_send()

            @pl.when(inside(part, zm if n < 2 else zp, n))
            def _():
                b_copy(part, c, n, 2, to_zp).wait_send()

    def multiply(source, phase, column, keeps, first_part):
        piece = 16 * l + mod(source + 4 * c, 16)
        top = mod(piece - c + 8, 32) // 4
        for g in range(4):
            u = jnp.where(top >= 3, top - 3 + g, jnp.where(g <= top, g, g + 4))
            t = 8 * third(phase) + u
            i = c + 4 * t
            d = mod(piece - i + 8, 32) - 8
            k = mod(i + d, 256)
            part = mod(k // 32 + l, 8) + first_part
            e = mod(column - k + 8, 16) - 8
            distance = mod(k - column, 16)
            present = (
                lax.shift_right_logical(a_mask[t], d + 8) & lax.shift_right_logical(b_mask[k], e + 8) & 1
            )
            weight = jnp.where(keeps(t) == d + e, present, 0).astype(jnp.float32)
            product = jnp.dot(
                abuf[phase, source, g],
                bbuf[part, distance // 4, distance % 4],
                preferred_element_type=jnp.float32,
            )
            total[u] += product * weight

    def own_keep(t):
        return keep[t]

    def other_keep(t):
        return keep_other[0, t]

    def add_sources(phase, column, keeps, first_part, wait):
        total[...] = jnp.zeros_like(total)

        def of_this_core(n, inner):
            multiply(row_of(mod(x + n, 4), mod(y + n // 4, 2), b), phase, column, keeps, first_part)
            return inner

        lax.fori_loop(0, 8, of_this_core, 0)

        def of_sibling(n, inner):
            source = row_of(mod(x + n, 4), mod(y + n // 4, 2), b1)
            if wait:
                got_a(source, phase, 0, 4, core_recv.at[phase, n])
            multiply(source, phase, column, keeps, first_part)
            return inner

        lax.fori_loop(0, 8, of_sibling, 0)

    def store_rows(put, count, row):
        def one(n, inner):
            put(n, total[row + n].astype(jnp.bfloat16))
            return inner

        lax.fori_loop(0, count, one, 0)

    def column_copy(index, device):
        return remote(
            leaving.at[index],
            parts.at[l, pl.ds(4 * y, 8)],
            p_send.at[index],
            p_recv.at[l],
            device,
        )

    to_other_column = {"row": r1, "layer": y}

    def middle_copy():
        return remote(swapped, parts.at[l, pl.ds(8 * l, 4)], p_send.at[2], p_recv.at[2], to_l)

    def bits(offsets, at):
        found = jnp.int32(0)
        for n in range(12):
            found += lax.shift_left(jnp.int32(1), offsets[n, at] + 8)
        return found

    def plan():
        def a_row(t, inner):
            a_mask[t] = bits(a_offsets, t)
            return inner

        lax.fori_loop(0, 24, a_row, 0)

        def b_row(n, inner):
            k = mod(n - 8, 256)
            b_mask[k] = bits(b_offsets, k)
            return inner

        lax.fori_loop(0, 111, b_row, 0)
        for t in range(12):
            before = jnp.int32(0)
            for n in range(t):
                before += jnp.where(owners[n] == owners[t], 1, 0)
            rank[t] = before

        def slot(at, inner):
            owner, place = at // 6, at % 6
            source, used = jnp.int32(0), jnp.int32(0)
            for t in range(12):
                here = jnp.where((owners[t] == owner) & (rank[t] == place), 1, 0)
                source += here * t
                used += here
            slot_source[at] = source
            slot_used[at] = used
            return inner

        lax.fori_loop(0, 24, slot, 0)

    own_copy(0).start()
    b_own_copy(1).start()
    b_own_copy(own_second).start()
    own_copy(1).start()
    b_own_copy(own_last).start()
    a_to_y(0)
    b_full_over_y().start()
    keep_copy = remote(keep_vector, keep_arrived, keep_sem.at[0], keep_sem.at[1], to_y)
    keep_copy.start()
    own_copy(0).wait()
    a_along_x(0, y)
    b_own_copy(1).wait()
    b_start(1)
    b_own_copy(own_second).wait()
    b_start(own_second)
    own_copy(1).wait()
    a_along_x(1, y)
    to_sibling(0, 0)
    plan()
    got_a(r1, 0, 0, 4, yy_recv.at[0])
    a_along_x(0, y1)
    edges_over_y(r, lambda copy: copy.start())
    b_full_over_y().wait_recv()
    b_start(other_full)
    a_to_y(1)
    to_sibling(0, 4)
    a_further(0, y)
    b_further(1)
    to_sibling(0, 1)
    to_sibling(0, 3)
    b_further(own_second)
    edges_over_y(r1, lambda copy: copy.wait_recv())
    b_start(other_edge)
    a_further(0, y1)
    to_sibling(0, 5)
    to_sibling(0, 7)
    got_a(r1, 1, 0, 4, yy_recv.at[1])
    a_along_x(1, y1)
    b_further(other_full)
    b_own_copy(own_last).wait()
    b_start(own_last)
    a_further(1, y)
    a_last(0, y)
    to_sibling(0, 2)
    a_last(0, y1)
    to_sibling(0, 6)
    to_sibling(1, 0)
    to_sibling(1, 4)
    b_last(1)
    b_last(own_second)
    b_further(other_edge)
    add_sources(0, r, own_keep, -y, True)

    @pl.when(y == l)
    def _():
        def put_here(n, value):
            parts[l, 4 * y + n] = value

        store_rows(put_here, 8, 0)

    @pl.when(y != l)
    def _():
        def put_own(n, value):
            leaving[1, n] = value

        store_rows(put_own, 8, 0)
        column_copy(1, to_l).start()

    to_sibling(1, 1)
    to_sibling(1, 3)
    a_further(1, y1)
    to_sibling(1, 5)
    to_sibling(1, 7)
    b_further(own_last)
    keep_copy.wait_recv()
    keep_local = pltpu.make_async_copy(keep_arrived, keep_other, local_sem.at[6])
    keep_local.start()
    keep_local.wait()
    b_last(other_full)
    b_last(other_edge)
    add_sources(0, r1, other_keep, 3 - 2 * y, False)

    def put_other(n, value):
        leaving[0, n] = value

    store_rows(put_other, 8, 0)
    column_copy(0, to_other_column).start()

    a_last(1, y)
    to_sibling(1, 2)
    a_last(1, y1)
    to_sibling(1, 6)
    b_last(own_last)
    add_sources(1, r, own_keep, -y, True)

    def put_middle(n, value):
        swapped[n] = value

    store_rows(put_middle, 4, 4 * l1)
    middle_copy().start()

    def put_middle_here(n, value):
        parts[l, 8 * l1 + n] = value

    store_rows(put_middle_here, 4, 4 * l)

    def part_arrived(layer):
        ref = parts.at[layer, pl.ds(4 * l, 8)]
        remote(leaving.at[0], ref, p_send.at[0], p_recv.at[layer], to_l).wait_recv()

    @pl.when(y == l)
    def _():
        part_arrived(l1)

    @pl.when(y != l)
    def _():
        part_arrived(0)
        part_arrived(1)

    remote(swapped, parts.at[l1, pl.ds(8 * l1, 4)], p_send.at[2], p_recv.at[2], to_l).wait_recv()

    def fill(owner):
        def one(n, inner):
            index = slot_source[owner * 6 + n]
            value = parts[0, index].astype(jnp.float32) + parts[1, index].astype(jnp.float32)
            slots[owner, n] = (value * slot_used[owner * 6 + n].astype(jnp.float32)).astype(jnp.bfloat16)
            return inner

        lax.fori_loop(0, 6, one, 0)

    def slot_copy(owner, index, device):
        return remote(slots.at[owner], out_ref.at[c], o_send.at[index], o_recv.at[index], device)

    for index, (owner, device) in enumerate(((z2, to_z2), (zp, to_zp), (zm, to_zm))):
        fill(owner)
        slot_copy(owner, index, device).start()
    fill(c)
    stay = pltpu.make_async_copy(slots.at[c], out_ref.at[c], local_sem.at[5])
    stay.start()
    for phase in range(2):
        ref = abuf.at[phase, pl.ds(0, 15)]
        remote(ref, ref, a_send.at[phase], core_recv.at[phase, 0], to_b).wait_send()
    keep_copy.wait_send()
    b_full_over_y().wait_send()
    edges_over_y(r, lambda copy: copy.wait_send())

    def all_sent(part, inner):
        b_sent(part)
        return inner

    lax.fori_loop(0, 5, all_sent, 0)
    column_copy(0, to_other_column).wait_send()

    @pl.when(y != l)
    def _():
        column_copy(1, to_l).wait_send()

    middle_copy().wait_send()
    stay.wait()
    for index, (owner, device, sender) in enumerate(((z2, to_z2, z2), (zp, to_zp, zm), (zm, to_zm, zp))):
        slot_copy(owner, index, device).wait_send()
        remote(slots.at[owner], out_ref.at[sender], o_send.at[index], o_recv.at[index], device).wait_recv()


def on_device(a_blocks, b_blocks, a_offsets, b_offsets, keep_offsets, owners):
    a_part = a_blocks.reshape(12, BLOCK, BLOCK)
    b_part = b_blocks.reshape(4, 8, BLOCK, BLOCK)
    keep = keep_offsets[:, 0, 0]
    smem = pl.BlockSpec(memory_space=pltpu.SMEM)
    anywhere = pl.BlockSpec(memory_space=pl.ANY)
    dma = pltpu.SemaphoreType.DMA
    block = (BLOCK, BLOCK)
    arrived = pl.pallas_call(
        kernel,
        out_shape=jax.ShapeDtypeStruct((4, 6, BLOCK, BLOCK), jnp.bfloat16),
        in_specs=[anywhere, anywhere, smem, smem, smem, smem, pl.BlockSpec(memory_space=pltpu.VMEM)],
        out_specs=anywhere,
        scratch_shapes=[
            pltpu.VMEM((2, 16, 4) + block, jnp.bfloat16),
            pltpu.VMEM((5, 4, 4) + block, jnp.bfloat16),
            pltpu.VMEM((8,) + block, jnp.float32),
            pltpu.VMEM((2, 12) + block, jnp.bfloat16),
            pltpu.VMEM((2, 8) + block, jnp.bfloat16),
            pltpu.VMEM((4,) + block, jnp.bfloat16),
            pltpu.VMEM((4, 6) + block, jnp.bfloat16),
            pltpu.VMEM((1, 24), jnp.int32),
            pltpu.SMEM((1, 24), jnp.int32),
            pltpu.SMEM((24,), jnp.int32),
            pltpu.SMEM((256,), jnp.int32),
            pltpu.SMEM((12,), jnp.int32),
            pltpu.SMEM((24,), jnp.int32),
            pltpu.SMEM((24,), jnp.int32),
            dma((7,)),
            dma((2,)),
            dma((2,)),
            dma((2,)),
            dma((2, 2, 2)),
            dma((2, 2, 2)),
            dma((2, 8)),
            dma((5,)),
            dma((5,)),
            dma((3, 5, 4)),
            dma((3, 5, 4)),
            dma((3,)),
            dma((3,)),
            dma((3,)),
            dma((3,)),
        ],
        compiler_params=pltpu.CompilerParams(
            collective_id=0, has_side_effects=True, vmem_limit_bytes=56 << 20
        ),
        cost_estimate=pl.CostEstimate(
            flops=192 * 2 * BLOCK**3, bytes_accessed=10 << 20, transcendentals=0
        ),
        name="banded_product",
    )(
        a_part,
        b_part,
        a_offsets[:, 0, :].T,
        b_offsets.T,
        keep,
        owners[:, 0, 0],
        keep.reshape(1, 24),
    )
    return arrived.reshape(1, 1, 1, 4, 6, BLOCK, BLOCK)


def solution(mesh):
    return jax.shard_map(
        on_device,
        mesh=mesh,
        in_specs=(
            P("row", "col", "layer", None, None, None),
            P("row", "col", "layer", None, None, None),
            P(None, "col", None),
            P(),
            P(None, "col", "row"),
            P("layer", "col", "row"),
        ),
        out_specs=P("row", "col", "layer", None, None, None, None),
        check_vma=False,
    )
```

time: 219 us -> 165 us (0.75)
  Pallas kernels: 207 us -> 158 us
  other arithmetic: 4.36 us -> 0 us
    pallas_call x1, Pallas kernels: 207 us -> 158 us  [on_device(): pl.pallas_call(kernel, out_shape=jax.ShapeDtypeStruct((4, 6, BLOCK, BLOCK...]
    reduce_sum x4 -> x0, other arithmetic: 3.68 us -> none  [the longest x1 1.3 us: on_device(): b_mask = jnp.sum(1 << b_offsets + 8, axis=1)]
    unnamed x1 -> x2, local copies, waits for them, and re-layouts: 3.86 us -> 5.15 us
where the time goes in v3:
time: 165 us; the launch traced here: 163 us
  Pallas kernels  158 us (96%)
  local copies, waits for them, and re-layouts  5.15 us (3%)
    pallas_call x1, Pallas kernels, on_device(): pl.pallas_call(kernel, out_shape=jax.ShapeDtypeStruct((4, 6, BLOCK, BLOCK...  158 us
    unnamed x2, local copies, waits for them, and re-layouts  5.15 us

profile of v3, /device:TPU:8, one launch (start us, length us, event | category | flops | bytes accessed | tf_op | source)
XLA Modules:
  0.0 163.2 jit_solution(9211390072337106620)
XLA Ops:
  0.0 1.3 copy.9
  1.3 158.0 %banded_product.1 = bf16[4,6,256,256]{3,2,1,0:T(8,128)(2,1)} custom-call(bf16[12,256,256]{2,1,0:T(8,128)(2,1)} %bitcast.15, bf16[4,8,256,256]{3,2,1,0:T(8,128)(2,1)} %bitcast.14, s32[12,24]{1,0:T(8,128)} %bitcast.13, s32[12,256]{1,0:T(8,128)} %bitcast.16, s32[24]{0:T(128)} %bitcast.17, s32[12]{0:T(128)} %bitcast.19, s32[1,24]{1,0:T(1,128)} %bitcast.18), custom_call_target="tpu_custom_call" | custom-call | flops 6442450944 | bytes 10485760 | tf_op jit(solution)/shard_map/banded_product/pallas_call | solution.py:493
  159.3 3.9 %copy.11 = bf16[1,1,1,4,6,256,256]{6,5,4,3,2,1,0:T(8,128)(2,1)} copy(bf16[1,1,1,4,6,256,256]{6,5,4,3,2,1,0:T(8,128)(2,1)} %bitcast.12) | data formatting | bytes 6291456

commit v4 on v3

--- a/solution.py
+++ b/solution.py
@@ -259,6 +259,27 @@
 
         lax.fori_loop(0, 8, of_sibling, 0)
 
+    def add_middle(first, count):
+        def place(at):
+            early = at + jnp.where(at >= 2, 1, 0) + jnp.where(at >= 5, 1, 0)
+            return jnp.where(at < 6, early, 4 * at - 22)
+
+        def of_this_core(at, inner):
+            n = place(at)
+            source = row_of(mod(x + n, 4), mod(y + n // 4, 2), b)
+            multiply(source, 1, r, own_keep, -y)
+            return inner
+
+        def of_sibling(at, inner):
+            n = place(at)
+            source = row_of(mod(x + n, 4), mod(y + n // 4, 2), b1)
+            got_a(source, 1, 0, 4, core_recv.at[1, n])
+            multiply(source, 1, r, own_keep, -y)
+            return inner
+
+        lax.fori_loop(first, first + count, of_this_core, 0)
+        lax.fori_loop(first, first + count, of_sibling, 0)
+
     def store_rows(put, count, row):
         def one(n, inner):
             put(n, total[row + n].astype(jnp.bfloat16))
@@ -283,19 +304,19 @@
     def bits(offsets, at):
         found = jnp.int32(0)
         for n in range(12):
-            found += lax.shift_left(jnp.int32(1), offsets[n, at] + 8)
+            found += lax.shift_left(jnp.int32(1), offsets(n, at) + 8)
         return found
 
     def plan():
         def a_row(t, inner):
-            a_mask[t] = bits(a_offsets, t)
+            a_mask[t] = bits(lambda n, at: a_offsets[n, 0, at], t)
             return inner
 
         lax.fori_loop(0, 24, a_row, 0)
 
         def b_row(n, inner):
             k = mod(n - 8, 256)
-            b_mask[k] = bits(b_offsets, k)
+            b_mask[k] = bits(lambda n, at: b_offsets[n, at], k)
             return inner
 
         lax.fori_loop(0, 111, b_row, 0)
@@ -333,12 +354,12 @@
     b_start(1)
     b_own_copy(own_second).wait()
     b_start(own_second)
-    own_copy(1).wait()
-    a_along_x(1, y)
     to_sibling(0, 0)
     plan()
     got_a(r1, 0, 0, 4, yy_recv.at[0])
     a_along_x(0, y1)
+    own_copy(1).wait()
+    a_along_x(1, y)
     edges_over_y(r, lambda copy: copy.start())
     b_full_over_y().wait_recv()
     b_start(other_full)
@@ -391,7 +412,6 @@
     a_further(1, y1)
     to_sibling(1, 5)
     to_sibling(1, 7)
-    b_further(own_last)
     keep_copy.wait_recv()
     keep_local = pltpu.make_async_copy(keep_arrived, keep_other, local_sem.at[6])
     keep_local.start()
@@ -405,13 +425,16 @@
 
     store_rows(put_other, 8, 0)
     column_copy(0, to_other_column).start()
-
+    b_further(own_last)
+
+    b_last(own_last)
+    total[...] = jnp.zeros_like(total)
+    add_middle(0, 6)
     a_last(1, y)
     to_sibling(1, 2)
     a_last(1, y1)
     to_sibling(1, 6)
-    b_last(own_last)
-    add_sources(1, r, own_keep, -y, True)
+    add_middle(6, 2)
 
     def put_middle(n, value):
         swapped[n] = value
@@ -536,7 +559,7 @@
     )(
         a_part,
         b_part,
-        a_offsets[:, 0, :].T,
+        a_offsets.transpose(2, 1, 0),
         b_offsets.T,
         keep,
         owners[:, 0, 0],

time: 165 us -> 162 us (0.982); the launches traced: 163 us -> 162 us
    unnamed x2 -> x1, local copies, waits for them, and re-layouts: 5.15 us -> 3.86 us
where the time goes in v4:
time: 162 us
  Pallas kernels  158 us (98%)
  local copies, waits for them, and re-layouts  3.86 us (2%)
    pallas_call x1, Pallas kernels, on_device(): pl.pallas_call(kernel, out_shape=jax.ShapeDtypeStruct((4, 6, BLOCK, BLOCK...  158 us
    unnamed x1, local copies, waits for them, and re-layouts  3.86 us

profile of v4, /device:TPU:8, one launch (start us, length us, event | category | flops | bytes accessed | tf_op | source)
XLA Modules:
  0.0 161.9 jit_solution(12344169416595003641)
XLA Ops:
  0.0 158.1 %banded_product.1 = bf16[4,6,256,256]{3,2,1,0:T(8,128)(2,1)} custom-call(bf16[12,256,256]{2,1,0:T(8,128)(2,1)} %bitcast.10, bf16[4,8,256,256]{3,2,1,0:T(8,128)(2,1)} %bitcast.9, s32[12,1,24]{2,1,0:T(1,128)} %bitcast.12, s32[12,256]{1,0:T(8,128)} %bitcast.11, s32[24]{0:T(128)} %bitcast.13, s32[12]{0:T(128)} %bitcast.15, s32[1,24]{1,0:T(1,128)} %bitcast.14), custom_call_target="tpu_custom_call" | custom-call | flops 6442450944 | bytes 10485760 | tf_op jit(solution)/shard_map/banded_product/pallas_call | solution.py:516
  158.1 3.9 %copy.8 = bf16[1,1,1,4,6,256,256]{6,5,4,3,2,1,0:T(8,128)(2,1)} copy(bf16[1,1,1,4,6,256,256]{6,5,4,3,2,1,0:T(8,128)(2,1)} %bitcast.8) | data formatting | bytes 6291456

commit v5 on v4

--- a/solution.py
+++ b/solution.py
@@ -462,22 +462,31 @@
 
     remote(swapped, parts.at[l1, pl.ds(8 * l1, 4)], p_send.at[2], p_recv.at[2], to_l).wait_recv()
 
-    def fill(owner):
-        def one(n, inner):
-            index = slot_source[owner * 6 + n]
-            value = parts[0, index].astype(jnp.float32) + parts[1, index].astype(jnp.float32)
-            slots[owner, n] = (value * slot_used[owner * 6 + n].astype(jnp.float32)).astype(jnp.bfloat16)
-            return inner
-
-        lax.fori_loop(0, 6, one, 0)
-
-    def slot_copy(owner, index, device):
-        return remote(slots.at[owner], out_ref.at[c], o_send.at[index], o_recv.at[index], device)
-
-    for index, (owner, device) in enumerate(((z2, to_z2), (zp, to_zp), (zm, to_zm))):
-        fill(owner)
-        slot_copy(owner, index, device).start()
-    fill(c)
+    def fill(owner, n):
+        index = slot_source[owner * 6 + n]
+        value = parts[0, index].astype(jnp.float32) + parts[1, index].astype(jnp.float32)
+        slots[owner, n] = (value * slot_used[owner * 6 + n].astype(jnp.float32)).astype(jnp.bfloat16)
+
+    def slot_copy(owner, n, index, device):
+        return remote(
+            slots.at[owner, n], out_ref.at[c, n], o_send.at[index, n], o_recv.at[index, n], device
+        )
+
+    targets = ((z2, to_z2, z2), (zp, to_zp, zm), (zm, to_zm, zp))
+
+    def send_slots(n, inner):
+        for index, (owner, device, _) in enumerate(targets):
+            fill(owner, n)
+            slot_copy(owner, n, index, device).start()
+        return inner
+
+    lax.fori_loop(0, 6, send_slots, 0)
+
+    def keep_slots(n, inner):
+        fill(c, n)
+        return inner
+
+    lax.fori_loop(0, 6, keep_slots, 0)
     stay = pltpu.make_async_copy(slots.at[c], out_ref.at[c], local_sem.at[5])
     stay.start()
     for phase in range(2):
@@ -500,9 +509,16 @@
 
     middle_copy().wait_send()
     stay.wait()
-    for index, (owner, device, sender) in enumerate(((z2, to_z2, z2), (zp, to_zp, zm), (zm, to_zm, zp))):
-        slot_copy(owner, index, device).wait_send()
-        remote(slots.at[owner], out_ref.at[sender], o_send.at[index], o_recv.at[index], device).wait_recv()
+
+    def end_slots(n, inner):
+        for index, (owner, device, sender) in enumerate(targets):
+            slot_copy(owner, n, index, device).wait_send()
+            remote(
+                slots.at[owner, n], out_ref.at[sender, n], o_send.at[index, n], o_recv.at[index, n], device
+            ).wait_recv()
+        return inner
+
+    lax.fori_loop(0, 6, end_slots, 0)
 
 
 def on_device(a_blocks, b_blocks, a_offsets, b_offsets, keep_offsets, owners):
@@ -546,8 +562,8 @@
             dma((3, 5, 4)),
             dma((3,)),
             dma((3,)),
-            dma((3,)),
-            dma((3,)),
+            dma((3, 6)),
+            dma((3, 6)),
         ],
         compiler_params=pltpu.CompilerParams(
             collective_id=0, has_side_effects=True, vmem_limit_bytes=56 << 20

time: 162 us -> 162 us (level)
  no operation moved by 1% of the time
where the time goes in v5:
time: 162 us
  Pallas kernels  158 us (98%)
  local copies, waits for them, and re-layouts  3.86 us (2%)
    pallas_call x1, Pallas kernels, on_device(): pl.pallas_call(kernel, out_shape=jax.ShapeDtypeStruct((4, 6, BLOCK, BLOCK...  158 us
    unnamed x1, local copies, waits for them, and re-layouts  3.86 us

profile of v5, /device:TPU:8, one launch (start us, length us, event | category | flops | bytes accessed | tf_op | source)
XLA Modules:
  0.0 162.1 jit_solution(18208356386651548310)
XLA Ops:
  0.0 158.3 %banded_product.1 = bf16[4,6,256,256]{3,2,1,0:T(8,128)(2,1)} custom-call(bf16[12,256,256]{2,1,0:T(8,128)(2,1)} %bitcast.10, bf16[4,8,256,256]{3,2,1,0:T(8,128)(2,1)} %bitcast.9, s32[12,1,24]{2,1,0:T(1,128)} %bitcast.12, s32[12,256]{1,0:T(8,128)} %bitcast.11, s32[24]{0:T(128)} %bitcast.13, s32[12]{0:T(128)} %bitcast.15, s32[1,24]{1,0:T(1,128)} %bitcast.14), custom_call_target="tpu_custom_call" | custom-call | flops 6442450944 | bytes 10485760 | tf_op jit(solution)/shard_map/banded_product/pallas_call | solution.py:532
  158.3 3.9 %copy.8 = bf16[1,1,1,4,6,256,256]{6,5,4,3,2,1,0:T(8,128)(2,1)} copy(bf16[1,1,1,4,6,256,256]{6,5,4,3,2,1,0:T(8,128)(2,1)} %bitcast.8) | data formatting | bytes 6291456

commit v6 on v5

--- a/solution.py
+++ b/solution.py
@@ -345,15 +345,18 @@
     own_copy(1).start()
     b_own_copy(own_last).start()
     a_to_y(0)
+    for index, device in ((0, to_xp), (1, to_xm)):
+        remote(
+            a_ref.at[pl.ds(8 * y, 4)], abuf.at[0, r], a_send.at[0], yx_recv.at[0, 0, index], device
+        ).start()
     b_full_over_y().start()
     keep_copy = remote(keep_vector, keep_arrived, keep_sem.at[0], keep_sem.at[1], to_y)
     keep_copy.start()
-    own_copy(0).wait()
-    a_along_x(0, y)
     b_own_copy(1).wait()
     b_start(1)
     b_own_copy(own_second).wait()
     b_start(own_second)
+    own_copy(0).wait()
     to_sibling(0, 0)
     plan()
     got_a(r1, 0, 0, 4, yy_recv.at[0])

time: 162 us -> 162 us (level)
  no operation moved by 1% of the time
where the time goes in v6:
time: 162 us
  Pallas kernels  158 us (98%)
  local copies, waits for them, and re-layouts  3.86 us (2%)
    pallas_call x1, Pallas kernels, on_device(): pl.pallas_call(kernel, out_shape=jax.ShapeDtypeStruct((4, 6, BLOCK, BLOCK...  158 us
    unnamed x1, local copies, waits for them, and re-layouts  3.86 us

profile of v6, /device:TPU:8, one launch (start us, length us, event | category | flops | bytes accessed | tf_op | source)
XLA Modules:
  0.0 162.2 jit_solution(10747540926299968574)
XLA Ops:
  0.0 158.3 %banded_product.1 = bf16[4,6,256,256]{3,2,1,0:T(8,128)(2,1)} custom-call(bf16[12,256,256]{2,1,0:T(8,128)(2,1)} %bitcast.10, bf16[4,8,256,256]{3,2,1,0:T(8,128)(2,1)} %bitcast.9, s32[12,1,24]{2,1,0:T(1,128)} %bitcast.12, s32[12,256]{1,0:T(8,128)} %bitcast.11, s32[24]{0:T(128)} %bitcast.13, s32[12]{0:T(128)} %bitcast.15, s32[1,24]{1,0:T(1,128)} %bitcast.14), custom_call_target="tpu_custom_call" | custom-call | flops 6442450944 | bytes 10485760 | tf_op jit(solution)/shard_map/banded_product/pallas_call | solution.py:535
  158.3 3.9 %copy.8 = bf16[1,1,1,4,6,256,256]{6,5,4,3,2,1,0:T(8,128)(2,1)} copy(bf16[1,1,1,4,6,256,256]{6,5,4,3,2,1,0:T(8,128)(2,1)} %bitcast.8) | data formatting | bytes 6291456
